TPU v7x, 128 devices: a whole 4x4x4 slice. The times are simulated.
128 devices in a mesh: outer: 16 (over z_lo, y, core), inner: 8 (over x, z_hi).
Axes of the slice: x: 4, y: 4, z: 4 (z_hi: 2, z_lo: 2; z = z_hi * 2 + z_lo), core: 2. Of those that a mesh axis runs over, the one named last changes fastest.
Arguments:
- tokens: bfloat16 [32768, 14848], P(('outer', 'inner')), may hold values from -24 to 24
- cotangent: bfloat16 [32768, 512], P(('outer', 'inner')), may hold values from -6 to 6
- lengths: int32 [8], replicated, may hold values from 1 to 4096
- frozen: bfloat16 [14848, 512], P(('outer', 'inner')), may hold values from -0.046875 to 0.046875
- down_weight: bfloat16 [14848, 64], P(('outer', 'inner')), may hold values from -0.046875 to 0.046875
- up_weight: bfloat16 [64, 512], replicated, may hold values from -0.75 to 0.75
Outputs:
- keys: bfloat16 [32768, 512], P(('outer', 'inner'))
- input_gradient: bfloat16 [32768, 14848], P(('outer', 'inner'))
- down_gradient: float32 [14848, 64], P(('outer', 'inner'))
- up_gradient: float32 [64, 512], replicated
All inputs are finite; a program needn't handle non-finite values.
Results may differ from a plain program's by a relative error of at most 0.0046.
Values may be sent and summed in bfloat16 or wider, within the bound.
A program may use at most 128 MiB of HBM per device.

v0:
```python
import jax
import jax.numpy as jnp
from jax import lax
from jax.sharding import PartitionSpec as P

SEQ_LEN = 4096


adapter_scale = 2.0


def on_device(tokens, cotangent, lengths, frozen, down_weight, up_weight):
    rows = tokens.shape[0]
    complete_weight, full_a = (
        lax.all_gather(frozen, ("outer", "inner"), axis=0, tiled=True),
        lax.all_gather(down_weight, ("outer", "inner"), axis=0, tiled=True),
    )
    reduced_rank_output = jnp.dot(tokens, full_a, preferred_element_type=jnp.float32).astype(
        jnp.bfloat16
    )
    keys = jnp.dot(
        tokens, complete_weight, preferred_element_type=jnp.float32
    ) + adapter_scale * jnp.dot(reduced_rank_output, up_weight, preferred_element_type=jnp.float32)
    first = lax.axis_index(("outer", "inner")) * rows
    global_pos = first + jnp.arange(rows, dtype=jnp.int32)
    seq_id = global_pos // SEQ_LEN
    position = global_pos % SEQ_LEN
    table = jnp.arange(lengths.shape[0], dtype=jnp.int32)
    own_length = jnp.sum(jnp.where(seq_id[:, None] == table[None, :], lengths[None, :], 0), axis=1)
    live = (position < own_length).astype(jnp.bfloat16)
    masked_tokens = cotangent * live[:, None]
    contract_product = (((1,), (1,)), ((), ()))
    expanded_output = lax.dot_general(
        masked_tokens, up_weight, contract_product, preferred_element_type=jnp.float32
    ).astype(jnp.bfloat16)
    back_w, adapter_backward = (complete_weight, full_a)
    input_gradient = lax.dot_general(
        masked_tokens, back_w, contract_product, preferred_element_type=jnp.float32
    ) + adapter_scale * lax.dot_general(
        expanded_output, adapter_backward, contract_product, preferred_element_type=jnp.float32
    )
    over_rows = (((0,), (0,)), ((), ()))
    down_product = adapter_scale * lax.dot_general(
        tokens, expanded_output, over_rows, preferred_element_type=jnp.float32
    )
    up_product = adapter_scale * lax.dot_general(
        reduced_rank_output, masked_tokens, over_rows, preferred_element_type=jnp.float32
    )
    summed_down, up_gradient = lax.psum((down_product, up_product), ("outer", "inner"))
    share = summed_down.shape[0] // lax.axis_size(("outer", "inner"))
    down_gradient = lax.dynamic_slice_in_dim(
        summed_down, lax.axis_index(("outer", "inner")) * share, share, 0
    )
    return (
        keys.astype(jnp.bfloat16),
        input_gradient.astype(jnp.bfloat16),
        down_gradient,
        up_gradient,
    )


def solution(mesh):
    return jax.shard_map(
        on_device,
        mesh=mesh,
        in_specs=(
            P(("outer", "inner"), None),
            P(("outer", "inner"), None),
            P(),
            P(("outer", "inner"), None),
            P(("outer", "inner"), None),
            P(),
        ),
        out_specs=(
            P(("outer", "inner"), None),
            P(("outer", "inner"), None),
            P(("outer", "inner"), None),
            P(),
        ),
        check_vma=False,
    )
```

profile of v0, /device:TPU:1, one launch (start us, length us, event | category | flops | bytes accessed | tf_op | source)
XLA Modules:
  0.0 875.9 jit_solution(9895064522823421655)
XLA Ops:
  7.2 0.0 copy-start
  7.2 0.0 all-gather.7.cloned.1.call-start
  7.2 0.7 all-gather.7.cloned.1.call-update
  7.9 0.0 all-reduce.3.cloned.1.call-start
  8.0 0.7 select_reduce_fusion
  8.7 1.2 convolution_convert_fusion
  10.0 6.5 fusion.2
  16.5 298.0 %all-gather.7.cloned.1.call-done = bf16[128,116,64]{1,2,0:T(8,128)(2,1)} async-done(((bf16[1,116,64]{1,2,0:T(8,128)(2,1)}), bf16[128,116,64]{1,2,0:T(8,128)(2,1)}) %all-gather.7.cloned.1.call-update) | async-done | bytes 1900560 | tf_op jit(solution)/shard_map/all_gather | solution.py:16
  314.4 4.3 copy.12
  318.7 4.7 reshape.48
  323.5 6.2 convolution_convert_fusion.1
  329.7 0.9 convolution_multiply_fusion.3
  330.6 0.0 all-reduce.3.cloned.1.call-update
  330.6 0.2 all-gather.5.cloned.1.call-start
  330.9 0.5 all-gather.5.cloned.1.call-update
  331.4 0.3 convolution_multiply_fusion.2
  331.6 152.9 %all-reduce.3.cloned.1.call-done = (f32[14848,64]{0,1:T(8,128)}, f32[64,512]{1,0:T(8,128)}) async-done(((f32[14848,64]{0,1:T(8,128)}, f32[64,512]{1,0:T(8,128)}), (f32[14848,64]{0,1:T(8,128)}, f32[64,512]{1,0:T(8,128)})) %all-reduce.3.cloned.1.call-update) | async-done | bytes 3932176 | tf_op jit(solution)/shard_map/psum | solution.py:49
  484.5 1.5 constant_dynamic-slice_fusion
  486.1 324.4 %all-gather.5.cloned.1.call-done = bf16[128,116,512]{2,1,0:T(8,128)(2,1)} async-done(((bf16[1,116,512]{2,1,0:T(8,128)(2,1)}), bf16[128,116,512]{2,1,0:T(8,128)(2,1)}) %all-gather.5.cloned.1.call-update) | async-done | bytes 15204368 | tf_op jit(solution)/shard_map/all_gather | solution.py:15
  810.5 20.4 %reshape.46 = bf16[14848,512]{1,0:T(8,128)(2,1)} reshape(bf16[128,116,512]{2,1,0:T(8,128)(2,1)} %all-gather.5.cloned.1.call-done) | data formatting | bytes 30408704
  830.9 18.5 %fusion.6 = f32[256,14848]{1,0:T(8,128)} fusion(bf16[14848,512]{1,0:T(8,128)(2,1)} %reshape.46, bf16[256,512]{1,0:T(8,128)(2,1)S(1)} %copy-done.4, bf16[256]{0:T(256)(128)(2,1)S(1)} %compare_convert_fusion), kind=kOutput, calls=%fused_computation.13 | convolution fusion | flops 3892445184 | bytes 30671360 | tf_op jit(solution)/shard_map/dot_general | solution.py:37
  849.4 12.4 %fusion.3 = bf16[256,512]{1,0:T(8,128)(2,1)} fusion(f32[256,512]{1,0:T(8,128)S(1)} %convolution_multiply_fusion.2, bf16[256,14848]{1,0:T(8,128)(2,1)} %param.6, bf16[14848,512]{1,0:T(8,128)(2,1)} %reshape.46), kind=kOutput, calls=%fused_computation.7 | convolution fusion | flops 3892576256 | bytes 23592960 | tf_op jit(solution)/shard_map/dot_general | solution.py:21
  861.8 6.9 fusion.1
  868.7 0.7 copy.15
  (13 shorter events, 0.0 us)
Async XLA Ops:
  7.2 1.6 copy-start
  7.2 307.3 %all-gather.7.cloned.1.call-start = ((), (), s32[]{:S(2)}) async-start(), calls=%async_computation.1 | async-start | bytes 2113536 | tf_op jit(solution)/shard_map/all_gather | solution.py:16
  7.9 476.6 %all-reduce.3.cloned.1.call-start = ((), (), s32[]{:S(2)}) async-start(), calls=%async_computation.2 | async-start | bytes 7864320 | tf_op jit(solution)/shard_map/psum | solution.py:49
  318.7 11.0 %copy-start.4 = (bf16[256,512]{1,0:T(8,128)(2,1)S(1)}, bf16[256,512]{1,0:T(8,128)(2,1)}, u32[]{:S(2)}) copy-start(bf16[256,512]{1,0:T(8,128)(2,1)} %param.7) | copy-start | bytes 786436
  323.4 507.5 %copy-start.3 = (bf16[14848,64]{0,1:T(8,128)(2,1)}, bf16[14848,64]{0,1:T(8,128)(2,1)S(1)}, u32[]{:S(2)}) copy-start(bf16[14848,64]{0,1:T(8,128)(2,1)S(1)} %reshape.48) | copy-start | bytes 5701636
  330.6 479.8 %all-gather.5.cloned.1.call-start = ((), (), s32[]{:S(2)}) async-start(), calls=%async_computation | async-start | bytes 15851520 | tf_op jit(solution)/shard_map/all_gather | solution.py:15
  849.4 12.4 %copy-start.2 = (f32[256,14848]{1,0:T(8,128)S(1)}, f32[256,14848]{1,0:T(8,128)}, u32[]{:S(2)}) copy-start(f32[256,14848]{1,0:T(8,128)} %fusion.6) | copy-start | bytes 45613060
  849.4 20.0 %copy-start.1 = (bf16[64,512]{1,0:T(8,128)(2,1)S(1)}, bf16[64,512]{1,0:T(8,128)(2,1)}, u32[]{:S(2)}) copy-start(bf16[64,512]{1,0:T(8,128)(2,1)} %param.11) | copy-start | bytes 196612
  861.8 6.9 copy-start.5
Sparse Core Ops, SparseCore 0:
  9.7 304.6 all-gather.6
  330.8 153.7 all-reduce.2
  486.2 324.2 all-gather.4
where the time goes:
time: 877 us; the launch traced here: 876 us
  waiting for transfers between devices  776 us (88%)
  matrix products  52.9 us (6%)
  local copies, waits for them, and re-layouts  31.6 us (4%)
  between operations  13.8 us (2%)
    all_gather x1, waiting for transfers between devices, on_device(): lax.all_gather(frozen, ('outer', 'inner'), axis=0, tiled=True)  324 us
    all_gather x1, waiting for transfers between devices, on_device(): lax.all_gather(down_weight, ('outer', 'inner'), axis=0, tiled=True)  298 us
    psum x1, waiting for transfers between devices, on_device(): lax.psum((down_product, up_product), ('outer', 'inner'))  153 us
    unnamed x15, local copies, waits for them, and re-layouts  25.8 us
    dot_general x1, matrix products, on_device(): lax.dot_general(masked_tokens, back_w, contract_product, preferred_elemen...  18.5 us
  transfers between devices with their start and end apart: 3, of which 3 were waited for; matrix products, arithmetic and copies ran while one was open for 1% of the time, Pallas kernels for 0%

commit v1 on v0

v1 whole, which is shorter than its diff:
```python
import jax
import jax.numpy as jnp
from jax import lax
from jax.experimental import pallas as pl
from jax.experimental.pallas import tpu as pltpu
from jax.sharding import PartitionSpec as P

MESH = pl.DeviceIdType.MESH
F32, BF16 = jnp.float32, jnp.bfloat16

D, KV, RANK, SEQ_LEN, ROWS, OWN = 14848, 512, 64, 4096, 256, 116
QUAD = 4 * OWN
STEP = 3712
adapter_scale = 2.0

STREAMS = (
    ("down", "zxy", 0, 64),
    ("w", "xyz", 0, 176),
    ("w", "yzx", 176, 176),
    ("w", "zxy", 352, 112),
)
SUMS = (("xyz", 0, 24, 8), ("yzx", 24, 24, 16), ("zxy", 48, 16, 8))
NSEM = 40
ALL = slice(None)


def comm_kernel(
    lengths, tokens_hbm, cot, frozen, down_t, up,
    w, dt, tokens, masked_out, raised_out, lowered_out, dgrad, ugrad,
    stage, quad, dt_raw, g, r, x0, xa, xb, xl, xr, y2, y3, v0, v1, v2, v3, v5,
    load_sem, quad_s, quad_r, ag_s, ag_r, sib_s, sib_r, rs_s, rs_r, up_s, up_r,
):
    outer, inner = lax.axis_index("outer"), lax.axis_index("inner")
    core = outer % 2
    me = {"x": inner // 2, "y": (outer // 2) % 4, "z": (inner % 2) * 2 + outer // 8}

    def device(core=core, **at):
        c = dict(me, **at)
        return ((c["z"] % 2) * 8 + c["y"] * 2 + core, c["x"] * 2 + c["z"] // 2)

    def step(axis, by):
        return (me[axis] + by) % 4

    sibling = device(core=1 - core)
    pending = []

    def send(src, dst, s, r_, to):
        copy = pltpu.make_async_remote_copy(
            src_ref=src, dst_ref=dst, send_sem=s, recv_sem=r_, device_id=to, device_id_type=MESH
        )
        copy.start()
        return copy

    load = pltpu.make_async_copy(tokens_hbm, tokens, load_sem)
    load.start()

    barrier = pltpu.get_barrier_semaphore()
    peers = [device(**{a: step(a, by)}) for a in "xyz" for by in (1, 2, 3)]
    xq = me["x"] + 1 - 2 * (me["x"] % 2)
    zq = step("z", 2)
    peers += [sibling, device(x=xq, z=zq)]
    for peer in peers:
        pl.semaphore_signal(barrier, inc=1, device_id=peer, device_id_type=MESH)

    kx, kz = me["x"] % 2, me["z"] // 2
    mine = kx * 2 + kz
    stage[...] = jnp.zeros_like(stage)
    for k in range(4):
        stage[k, 0:OWN, :] = frozen[:, 128 * k : 128 * (k + 1)]
    at_home = (me["z"] % 2, me["y"], core, me["x"], me["z"] // 2)
    dt_raw[at_home] = jnp.concatenate([down_t[...], jnp.zeros((RANK, 128 - OWN), BF16)], axis=1)

    pl.semaphore_wait(barrier, len(peers))

    quad_copies = []
    for n, (dx, dz) in enumerate(((1, 0), (0, 1), (1, 1))):
        tx, tz = (kx + dx) % 2, (kz + dz) % 2
        to = device(x=xq if dx else me["x"], z=zq if dz else me["z"])
        quad_copies.append(
            send(stage.at[tx * 2 + tz], quad.at[mine], quad_s.at[n], quad_r.at[n], to)
        )
    quad[mine] = stage[mine]

    first = (outer % 2 * 8 + inner) * ROWS
    length = lengths[outer // 2]
    position = first + lax.broadcasted_iota(jnp.int32, (ROWS, KV), 0)
    live = jnp.where(position < length, 1.0, 0.0).astype(BF16)
    masked = cot[...] * live
    masked_out[...] = masked
    contract = (((1,), (1,)), ((), ()))
    raised = lax.dot_general(masked, up[...], contract, preferred_element_type=F32).astype(BF16)
    raised2 = raised * jnp.asarray(adapter_scale, BF16)
    raised_out[...] = raised2
    raised2_t = raised2.astype(F32).T.astype(BF16)

    def at_of(kind, at, r0, n):
        x, y, z, c = at["x"], at["y"], at["z"], at["core"]
        whole = lambda v: isinstance(v, slice)
        zhi, zlo = (ALL, ALL) if whole(z) else (z // 2, z % 2)
        rows = pl.ds(r0, n)
        if kind == "down":
            return dt_raw.at[zlo, y, c, x, zhi, rows, :]
        xhi, xlo = (ALL, ALL) if whole(x) else (x // 2, x % 2)
        return w.at[xlo, zhi, zlo, y, c, xhi, rows, :]

    streams = []

    class Stream:
        def __init__(self, n):
            self.n = n
            self.kind, (self.a, self.b, self.c), self.r0, self.rows = STREAMS[n]
            self.cut = self.rows // 32 * 16
            self.copies = {}
            self.sem = 0
            self.sib_sem = 0
            self.sib_copies = []

        def ref(self, at, part=None):
            r0, rows = self.r0, self.rows
            if part == 0:
                rows = self.cut
            elif part == 1:
                r0, rows = r0 + self.cut, rows - self.cut
            return at_of(self.kind, {**me, "core": core, **at}, r0, rows)

        def go(self, key, axis, by, at, part=None):
            ref = self.ref(at, part)
            copy = send(
                ref, ref, ag_s.at[self.n, self.sem], ag_r.at[self.n, self.sem],
                device(**{axis: step(axis, by)}),
            )
            self.sem += 1
            self.copies[key] = copy

        def sib(self, at):
            ref = self.ref(at)
            self.sib_copies.append(
                send(ref, ref, sib_s.at[self.n, self.sib_sem], sib_r.at[self.n, self.sib_sem], sibling)
            )
            self.sib_sem += 1

        def open(self, name, axis, at):
            self.go(name + "R", axis, 1, {**at, axis: me[axis]})
            self.go(name + "L", axis, -1, {**at, axis: me[axis]})

        def forward(self, name, axis, at):
            self.copies[name + "R"].wait_recv()
            self.go(name + "r", axis, 1, {**at, axis: step(axis, -1)}, 0)
            self.copies[name + "L"].wait_recv()
            self.go(name + "l", axis, -1, {**at, axis: step(axis, 1)}, 1)

        def close(self, name):
            self.copies[name + "r"].wait_recv()
            self.copies[name + "l"].wait_recv()

        def open1(self):
            self.open("1", self.a, {})

        def forward1(self):
            self.forward("1", self.a, {})

        def close1(self):
            self.close("1")
            at = {self.a: ALL}
            self.open("2", self.b, at)
            self.sib(at)

        def sub(self, j):
            return {self.a: ALL, self.b: step(self.b, (0, -1, 1, 2)[j])}

        def open3(self, j):
            self.open(f"3{j}", self.c, self.sub(j))

        def forward2(self):
            self.forward("2", self.b, {self.a: ALL})
            self.sib(self.sub(1))
            self.sib(self.sub(2))

        def close2(self):
            self.close("2")
            self.sib(self.sub(3))

        def forward3(self, j):
            self.forward(f"3{j}", self.c, self.sub(j))
            self.sib({**self.sub(j), self.c: step(self.c, -1)})
            self.sib({**self.sub(j), self.c: step(self.c, 1)})

        def close3(self, j):
            self.close(f"3{j}")
            self.sib({**self.sub(j), self.c: step(self.c, 2)})

        def end_sib(self):
            for copy in self.sib_copies:
                copy.wait_recv()

        def end(self):
            for copy in list(self.copies.values()) + self.sib_copies:
                copy.wait_send()

    streams = [Stream(n) for n in range(len(STREAMS))]

    x0_copies = []

    def owners(c):
        load_once(c)
        for n in range(0, STEP, 256):
            m = min(256, STEP - n)
            g[:, n : n + m] = jnp.dot(
                raised2_t, tokens[:, STEP * c + n : STEP * c + n + m], preferred_element_type=F32
            )
        for i in range(32):
            o, x, zhi = i // 8, i // 2 % 4, i % 2
            piece = g[:, OWN * i : OWN * (i + 1)]
            r[c // 2, 2 * (c % 2) + o // 2, o % 2, x, zhi, :, 0:OWN] = piece
            r[c // 2, 2 * (c % 2) + o // 2, o % 2, x, zhi, :, OWN:128] = jnp.zeros((RANK, 128 - OWN), F32)
        zlo, y = c // 2, pl.ds(2 * (c % 2), 2)
        x0_copies.append(
            send(r.at[zlo, y, 1 - core], x0.at[zlo, y], rs_s.at[0, c], rs_r.at[0, c], sibling)
        )

    def load_once(c):
        if c == 0:
            load.wait()

    def add_sibling(c):
        x0_copies[c].wait_recv()
        for y in range(2 * (c % 2), 2 * (c % 2) + 2):
            for x in range(4):
                r[c // 2, y, core, x] = r[c // 2, y, core, x] + x0[c // 2, y, x]

    def r_at(at, r0, n):
        z = at["z"]
        zhi, zlo = (ALL, ALL) if isinstance(z, slice) else (z // 2, z % 2)
        return r.at[zlo, at["y"], core, at["x"], zhi, pl.ds(r0, n), :]

    class Sum:
        def __init__(self, n):
            self.n = n
            (self.a, self.b, self.c), self.r0, self.rows, self.cut = SUMS[n]
            self.free = {self.a: ALL, self.b: ALL, self.c: ALL}
            self.sends = []

        def go(self, src, dst, k, axis, by):
            copy = send(src, dst, rs_s.at[1 + self.n, k], rs_r.at[1 + self.n, k], device(**{axis: step(axis, by)}))
            self.sends.append(copy)
            return copy

        def at(self, by, half=None):
            r0, rows = self.r0, self.rows
            if half == 0:
                rows = self.cut
            elif half == 1:
                r0, rows = r0 + self.cut, rows - self.cut
            return r_at({**self.free, self.a: step(self.a, by)}, r0, rows)

        def first(self):
            self.ca = self.go(self.at(2, 0), xa[self.n], 0, self.a, 1)
            self.cb = self.go(self.at(2, 1), xb[self.n], 1, self.a, -1)

        def second(self):
            self.ca.wait_recv()
            ref = self.at(1, 0)
            ref[...] = ref[...] + xa[self.n][...]
            self.cl = self.go(self.at(1), xl[self.n], 2, self.a, 1)
            self.cb.wait_recv()
            ref = self.at(-1, 1)
            ref[...] = ref[...] + xb[self.n][...]
            self.cr = self.go(self.at(-1), xr[self.n], 3, self.a, -1)

        def third(self):
            self.cl.wait_recv()
            self.cr.wait_recv()
            ref = self.at(0)
            ref[...] = ref[...] + xl[self.n][...] + xr[self.n][...]
            self.k = []
            for j, by in enumerate((1, -1, 2)):
                src = r_at({**self.free, self.a: me[self.a], self.b: step(self.b, by)}, self.r0, self.rows)
                self.k.append(self.go(src, y2[self.n].at[j], 4 + j, self.b, by))

        def fourth(self):
            for copy in self.k:
                copy.wait_recv()
            ref = r_at({**me, self.c: ALL}, self.r0, self.rows)
            ref[...] = ref[...] + y2[self.n][0] + y2[self.n][1] + y2[self.n][2]
            self.k = []
            for j, by in enumerate((1, -1, 2)):
                src = r_at({**me, self.c: step(self.c, by)}, self.r0, self.rows)
                self.k.append(self.go(src, y3[self.n].at[j], 7 + j, self.c, by))

        def fifth(self):
            for copy in self.k:
                copy.wait_recv()
            own = r_at(me, self.r0, self.rows)
            total = own[...] + y3[self.n][0] + y3[self.n][1] + y3[self.n][2]
            dgrad[self.r0 : self.r0 + self.rows, :] = total[:, 0:OWN]

        def end(self):
            for copy in self.sends:
                copy.wait_send()

    sums = [Sum(n) for n in range(3)]

    up_copies = []

    def up_send(src, dst, k, to):
        copy = send(src, dst, up_s.at[k], up_r.at[k], to)
        up_copies.append(copy)
        return copy

    def rows_at(c, z=None):
        return pl.ds(pl.multiple_of(c * 32, 8), 32) if z is None else pl.ds(pl.multiple_of(c * 32 + z * 8, 8), 8)

    state = {}

    def lowered_and_up():
        def chunk(c, carry):
            for i in range(32):
                o, x, zhi = i // 8, i // 2 % 4, i % 2
                piece = dt_raw[c // 2, 2 * (c % 2) + o // 2, o % 2, x, zhi]
                dt[:, OWN * i + STEP * c : OWN * (i + 1) + STEP * c] = piece[:, 0:OWN]
            return carry

        for c in range(4):
            chunk(c, 0)
        total = jnp.zeros((ROWS, RANK), F32)
        for c in range(29):
            total += lax.dot_general(
                tokens[:, 512 * c : 512 * (c + 1)], dt[:, 512 * c : 512 * (c + 1)], contract,
                preferred_element_type=F32,
            )
        lowered2 = total.astype(BF16) * jnp.asarray(adapter_scale, BF16)
        lowered_out[...] = lowered2
        lowered2_t = lowered2.astype(F32).T.astype(BF16)
        ugrad[...] = jnp.dot(lowered2_t, masked_out[...], preferred_element_type=F32)
        state["k"] = [up_send(ugrad.at[rows_at(1 - core)], v0, 0, sibling)]

    def wait_up():
        for copy in state["k"]:
            copy.wait_recv()

    def up_z():
        wait_up()
        own = rows_at(core)
        v0[...] = v0[...] + ugrad[own, :]
        state["k"] = []
        for j, by in enumerate((1, 2, 3)):
            z = step("z", by)
            src = v0.at[pl.ds(pl.multiple_of(z * 8, 8), 8)]
            state["k"].append(up_send(src, v1.at[j], 1 + j, device(z=z)))

    def up_x():
        wait_up()
        own = v0[pl.ds(pl.multiple_of(me["z"] * 8, 8), 8), :]
        v2[me["x"]] = own + v1[0] + v1[1] + v1[2]
        state["k"] = [
            up_send(v2.at[me["x"]], v2.at[me["x"]], 4 + j, device(x=step("x", by)))
            for j, by in enumerate((1, 2, 3))
        ]

    def up_y():
        wait_up()
        v3[me["y"]] = v2[0] + v2[1] + v2[2] + v2[3]
        state["k"] = [
            up_send(v3.at[me["y"]], v3.at[me["y"]], 7 + j, device(y=step("y", by)))
            for j, by in enumerate((1, 2, 3))
        ]

    def up_gather():
        wait_up()
        own = rows_at(core, me["z"])
        ugrad[own, :] = v3[0] + v3[1] + v3[2] + v3[3]
        ref = ugrad.at[own]
        state["k"] = [up_send(ref, ref, 10 + j, device(z=step("z", by))) for j, by in enumerate((1, 2, 3))]

    def up_pair():
        wait_up()
        state["k"] = [up_send(ugrad.at[rows_at(core)], v5, 13, sibling)]

    owners(0)
    for copy in quad_copies:
        copy.wait_recv()
    piece = jnp.concatenate([quad[k, 0:OWN, :].astype(F32) for k in range(4)], axis=0).astype(BF16)
    w[kx, kz, me["z"] % 2, me["y"], core, me["x"] // 2] = piece
    for s in streams:
        s.open1()
    owners(1)
    for s in streams:
        s.forward1()
    owners(2)
    for s in streams:
        s.close1()
    for s in streams:
        s.open3(0)
    owners(3)
    for s in streams:
        s.forward2()
    for c in range(4):
        add_sibling(c)
    for s in sums:
        s.first()
    for s in streams:
        s.open3(1)
        s.open3(2)
    for s in streams:
        s.close2()
    for s in sums:
        s.second()
    for s in streams:
        s.open3(3)
    for s in streams:
        s.forward3(0)
    for s in sums:
        s.third()
    for s in streams:
        s.forward3(1)
    for s in sums:
        s.fourth()
    for s in streams:
        s.forward3(2)
    for s in sums:
        s.fifth()
    down = streams[0]
    down.forward3(3)
    for j in range(4):
        down.close3(j)
    down.end_sib()
    lowered_and_up()
    for s in streams[1:]:
        s.forward3(3)
    up_z()
    for s in streams[1:]:
        s.close3(0)
    up_x()
    for s in streams[1:]:
        s.close3(1)
    up_y()
    for s in streams[1:]:
        s.close3(2)
    up_gather()
    for s in streams[1:]:
        s.close3(3)
    up_pair()
    for s in streams[1:]:
        s.end_sib()
    wait_up()
    up_copies[0].wait_send()
    ugrad[rows_at(1 - core), :] = v5[...]
    for s in streams:
        s.end()
    for s in sums:
        s.end()
    for copy in quad_copies + x0_copies + up_copies[1:]:
        copy.wait_send()


def product_kernel(
    up, w, dt, tokens, masked, raised2, lowered2, dgrad_in, ugrad_in,
    keys, ig_hbm, dgrad, ugrad,
    ig, store_sem,
):
    width = 512
    steps = D // width

    def store(c):
        at = pl.ds(pl.multiple_of(c * width, 128), width)
        return pltpu.make_async_copy(ig.at[:, at], ig_hbm.at[:, at], store_sem.at[c])

    dgrad[...] = dgrad_in[...]
    ugrad[...] = ugrad_in[...]
    contract = (((1,), (1,)), ((), ()))

    def body(c, total):
        at = pl.ds(pl.multiple_of(c * width, 128), width)
        wc = jnp.concatenate([w[k, at, :] for k in range(4)], axis=1)
        out = lax.dot_general(masked[...], wc, contract, preferred_element_type=F32)
        out += jnp.dot(raised2[...], dt[:, at], preferred_element_type=F32)
        ig[:, at] = out.astype(BF16)
        store(c).start()
        return total + jnp.dot(tokens[:, at], wc, preferred_element_type=F32)

    total = jnp.dot(lowered2[...], up[...], preferred_element_type=F32)
    total = lax.fori_loop(0, steps, body, total)
    keys[...] = total.astype(BF16)
    for c in range(steps):
        store(c).wait()


def on_device(tokens, cotangent, lengths, frozen, down_weight, up_weight):
    vmem = pl.BlockSpec(memory_space=pltpu.VMEM)
    anywhere = pl.BlockSpec(memory_space=pl.ANY)
    in_hbm = lambda array: pltpu.with_memory_space_constraint(array, pltpu.HBM)
    down_t = down_weight.T
    axis_dims = {"x": (4,), "y": (4,), "z": (2, 2)}

    def free_dims(first):
        dims = []
        for name, axis in (("z", 2), ("y", 4), ("x", 4), ("z", 2)):
            if name != first:
                dims.append(axis)
        return tuple(dims)

    def buffers(shape):
        return [pltpu.VMEM(shape(n), F32) for n in range(3)]

    def cdims(axis):
        return (2, 2) if axis == "z" else (4,)

    scratch = [
        pltpu.VMEM((4, 128, 128), BF16),
        pltpu.VMEM((4, 128, 128), BF16),
        pltpu.VMEM((2, 4, 2, 4, 2, RANK, 128), BF16),
        pltpu.VMEM((RANK, STEP), F32),
        pltpu.VMEM((2, 4, 2, 4, 2, RANK, 128), F32),
        pltpu.VMEM((2, 4, 4, 2, RANK, 128), F32),
        buffers(lambda n: free_dims(SUMS[n][0][0]) + (SUMS[n][3], 128)),
        buffers(lambda n: free_dims(SUMS[n][0][0]) + (SUMS[n][2] - SUMS[n][3], 128)),
        buffers(lambda n: free_dims(SUMS[n][0][0]) + (SUMS[n][2], 128)),
        buffers(lambda n: free_dims(SUMS[n][0][0]) + (SUMS[n][2], 128)),
        buffers(lambda n: (3,) + cdims(SUMS[n][0][2]) + (SUMS[n][2], 128)),
        buffers(lambda n: (3, SUMS[n][2], 128)),
        pltpu.VMEM((32, KV), F32),
        pltpu.VMEM((3, 8, KV), F32),
        pltpu.VMEM((4, 8, KV), F32),
        pltpu.VMEM((4, 8, KV), F32),
        pltpu.VMEM((32, KV), F32),
        pltpu.SemaphoreType.DMA,
        pltpu.SemaphoreType.DMA((3,)),
        pltpu.SemaphoreType.DMA((3,)),
        pltpu.SemaphoreType.DMA((4, NSEM)),
        pltpu.SemaphoreType.DMA((4, NSEM)),
        pltpu.SemaphoreType.DMA((4, 16)),
        pltpu.SemaphoreType.DMA((4, 16)),
        pltpu.SemaphoreType.DMA((4, 10)),
        pltpu.SemaphoreType.DMA((4, 10)),
        pltpu.SemaphoreType.DMA((14,)),
        pltpu.SemaphoreType.DMA((14,)),
    ]
    gathered = pl.pallas_call(
        comm_kernel,
        out_shape=(
            pltpu.VMEM((2, 2, 2, 4, 2, 2, QUAD, 128), BF16),
            pltpu.VMEM((RANK, D), BF16),
            pltpu.VMEM((ROWS, D), BF16),
            pltpu.VMEM((ROWS, KV), BF16),
            pltpu.VMEM((ROWS, RANK), BF16),
            pltpu.VMEM((ROWS, RANK), BF16),
            pltpu.VMEM((RANK, OWN), F32),
            pltpu.VMEM((RANK, KV), F32),
        ),
        in_specs=[pl.BlockSpec(memory_space=pltpu.SMEM), anywhere] + [vmem] * 4,
        out_specs=(vmem,) * 8,
        scratch_shapes=scratch,
        compiler_params=pltpu.CompilerParams(
            collective_id=0, has_side_effects=True, vmem_limit_bytes=20 * 1024 * 1024
        ),
        name="gather_and_sum",
    )(lengths, in_hbm(tokens), cotangent, frozen, down_t, up_weight)
    gathered = (gathered[0].reshape(4, D, 128),) + tuple(gathered[1:])
    gathered = [pltpu.with_memory_space_constraint(part, pltpu.VMEM) for part in gathered]
    keys, ig, dgrad, ugrad = pl.pallas_call(
        product_kernel,
        out_shape=(
            jax.ShapeDtypeStruct((ROWS, KV), BF16),
            jax.ShapeDtypeStruct((ROWS, D), BF16),
            jax.ShapeDtypeStruct((RANK, OWN), F32),
            jax.ShapeDtypeStruct((RANK, KV), F32),
        ),
        in_specs=[vmem] * 9,
        out_specs=(vmem, anywhere, vmem, vmem),
        scratch_shapes=[
            pltpu.VMEM((ROWS, D), BF16),
            pltpu.SemaphoreType.DMA((D // 512,)),
        ],
        compiler_params=pltpu.CompilerParams(vmem_limit_bytes=16 * 1024 * 1024),
        name="products",
    )(up_weight, *gathered)
    return keys, ig, dgrad.T, ugrad


def solution(mesh):
    return jax.shard_map(
        on_device,
        mesh=mesh,
        in_specs=(
            P(("outer", "inner"), None),
            P(("outer", "inner"), None),
            P(),
            P(("outer", "inner"), None),
            P(("outer", "inner"), None),
            P(),
        ),
        out_specs=(
            P(("outer", "inner"), None),
            P(("outer", "inner"), None),
            P(("outer", "inner"), None),
            P(),
        ),
        check_vma=False,
    )
```

time: 877 us -> 109 us (0.12)
  waiting for transfers between devices: 776 us -> 0 us
  Pallas kernels: 0 us -> 104 us
  matrix products: 52.9 us -> 0 us
  local copies, waits for them, and re-layouts: 31.6 us -> 4.05 us
  between operations: 13.8 us -> 0.65 us
    all_gather x2 -> x0, waiting for transfers between devices: 622 us -> none  [the longest x1 324 us: on_device(): lax.all_gather(frozen, ('outer', 'inner'), axis=0, tiled=True)]
    psum x1 -> x0, waiting for transfers between devices: 153 us -> none  [on_device(): lax.psum((down_product, up_product), ('outer', 'inner'))]
    pallas_call x0 -> x2, Pallas kernels: none -> 104 us  [the longest x1 86.9 us: on_device(): pl.pallas_call(comm_kernel, out_shape=(pltpu.VMEM((2, 2, 2, 4, 2, 2, QUAD...]
    dot_general x8 -> x0, matrix products: 52.9 us -> none  [the longest x1 18.5 us: on_device(): lax.dot_general(masked_tokens, back_w, contract_product, preferred_elemen...]
    unnamed x15 -> x10, local copies, waits for them, and re-layouts: 25.8 us -> 4.05 us
  transfers between devices with their start and end apart: 3 -> 0, of which waited for: 3 -> 0; matrix products, arithmetic and copies ran while one was open for 1% -> 0% of each run, Pallas kernels for 0% -> 0%
where the time goes in v1:
time: 109 us
  Pallas kernels  104 us (95%)
  local copies, waits for them, and re-layouts  4.05 us (4%)
    pallas_call x1, Pallas kernels, on_device(): pl.pallas_call(comm_kernel, out_shape=(pltpu.VMEM((2, 2, 2, 4, 2, 2, QUAD...  86.9 us
    pallas_call x1, Pallas kernels, on_device(): pl.pallas_call(product_kernel, out_shape=(jax.ShapeDtypeStruct((ROWS, KV)...  17.2 us
    unnamed x10, local copies, waits for them, and re-layouts  4.05 us

profile of v1, /device:TPU:1, one launch (start us, length us, event | category | flops | bytes accessed | tf_op | source)
XLA Modules:
  0.0 108.8 jit_solution(13407799572707114727)
XLA Ops:
  0.6 0.0 copy-start
  0.6 0.8 copy-done
  1.5 0.0 copy-start.1
  1.5 0.9 copy-done.1
  2.4 0.0 copy-start.2
  2.4 0.9 copy-done.2
  3.3 0.0 copy-start.3
  3.3 0.7 copy-done.3
  4.0 0.0 copy-start.4
  4.0 0.7 copy-done.4
  4.7 86.9 %gather_and_sum.1 = (bf16[2,2,2,4,2,2,464,128]{7,6,5,4,3,2,1,0:T(8,128)(2,1)S(1)}, bf16[64,14848]{1,0:T(8,128)(2,1)S(1)}, bf16[256,14848]{1,0:T(8,128)(2,1)S(1)}...) custom-call(s32[8]{0:T(128)S(1)} %copy-done.4, ...), custom_call_target="tpu_custom_call" | custom-call | tf_op jit(solution)/shard_map/gather_and_sum/pallas_call | solution.py:538
  91.6 17.2 %products.1 = (bf16[256,512]{1,0:T(8,128)(2,1)}, bf16[256,14848]{1,0:T(8,128)(2,1)}, f32[64,116]{1,0:T(8,128)}, f32[64,512]{1,0:T(8,128)}) custom-call(bf16[64,512]{1,0:T(8,128)(2,1)S(1)} %copy-done, bf16[4,14848,128]{2,1,0:T(8,128)(2,1)S(1)} %bitcast.3, bf16[64,14848]{1,0:T(8,128)(2,1)S(1)} %get-tuple-element.17.dt, ...), custom_call_target="tpu_custom_call" | custom-call | tf_op jit(solution)/shard_map/products/pallas_call | solution.py:560
Async XLA Ops:
  0.6 0.8 copy-start
  1.5 0.9 copy-start.1
  2.4 0.9 copy-start.2
  3.3 0.7 copy-start.3
  4.0 0.7 copy-start.4

commit v2 on v0

v2 whole, which is shorter than its diff:
```python
import jax
import jax.numpy as jnp
from jax import lax
from jax.experimental import pallas as pl
from jax.experimental.pallas import tpu as pltpu
from jax.sharding import PartitionSpec as P

MESH = pl.DeviceIdType.MESH
F32, BF16 = jnp.float32, jnp.bfloat16

D, KV, RANK, SEQ_LEN, ROWS, OWN = 14848, 512, 64, 4096, 256, 116
QUAD = 4 * OWN
STEP = 3712
adapter_scale = 2.0

STREAMS = {
    "D": ("down", "yzx", 0, 64),
    "Z": ("w", "xyz", 0, 192),
    "X": ("w", "zyx", 192, 128),
    "Y": ("w", "xzy", 320, 144),
}
SUMS = (("xyz", 0, 24, 8), ("yzx", 24, 24, 16), ("zxy", 48, 16, 8))
ALL = slice(None)


def comm_kernel(
    lengths_hbm, tokens_hbm, cot_hbm, frozen_hbm, down_hbm, up_hbm,
    ig, keys, dgrad, ugrad,
    w, dt, tokens, lengths, cot, frozen, down_t, up, masked, total,
    stage, quad, dt_raw, g, r, x0, sa, sb, sl, sr, xa, xb, xl, xr, y2, y3, u0, u1, u2, u3,
    load_sem, quad_s, quad_r, ag_s, ag_r, sib_s, sib_r, rs_s, rs_r, up_s, up_r,
):
    outer, inner = lax.axis_index("outer"), lax.axis_index("inner")
    core = outer % 2
    me = {"x": inner // 2, "y": (outer // 2) % 4, "z": (inner % 2) * 2 + outer // 8}
    side = {a: 1 - 2 * (me[a] % 2) for a in "xyz"}

    def device(core=core, **at):
        c = dict(me, **at)
        return ((c["z"] % 2) * 8 + c["y"] * 2 + core, c["x"] * 2 + c["z"] // 2)

    def step(axis, by):
        return (me[axis] + by + 4) % 4

    sibling = device(core=1 - core)

    def send(src, dst, s, r_, to):
        copy = pltpu.make_async_remote_copy(
            src_ref=src, dst_ref=dst, send_sem=s, recv_sem=r_, device_id=to, device_id_type=MESH
        )
        copy.start()
        return copy

    barrier = pltpu.get_barrier_semaphore()
    peers = [device(**{a: step(a, by)}) for a in "xyz" for by in (1, 2, 3)]
    xq = me["x"] + 1 - 2 * (me["x"] % 2)
    zq = step("z", 2)
    peers += [device(core=1 - core, z=step("z", by)) for by in range(4)]
    peers += [device(x=xq, z=zq)]
    for peer in peers:
        pl.semaphore_signal(barrier, inc=1, device_id=peer, device_id_type=MESH)

    loads = []
    quarters = [pl.ds(STEP * c, STEP) for c in range(4)]
    for n, (src, dst) in enumerate((
        (frozen_hbm, frozen), (down_hbm, down_t), (cot_hbm, cot), (up_hbm, up),
        (lengths_hbm, lengths),
    ) + tuple((tokens_hbm.at[:, at], tokens.at[:, at]) for at in quarters)):
        loads.append(pltpu.make_async_copy(src, dst, load_sem.at[n]))
        loads[-1].start()

    kx, kz = me["x"] % 2, me["z"] // 2
    mine = kx * 2 + kz
    quad_copies = []

    def fill_stage():
        loads[0].wait()
        stage[...] = jnp.zeros_like(stage)
        for k in range(4):
            stage[k, 0:OWN, :] = frozen[:, 128 * k : 128 * (k + 1)]
        at_home = (me["z"] % 2, me["y"], core, me["x"], me["z"] // 2)
        loads[1].wait()
        dt_raw[at_home] = jnp.concatenate([down_t[...], jnp.zeros((RANK, 128 - OWN), BF16)], axis=1)

    def exchange():
        pl.semaphore_wait(barrier, len(peers))
        for n, (dx, dz) in enumerate(((1, 0), (0, 1), (1, 1))):
            tx, tz = (kx + dx) % 2, (kz + dz) % 2
            to = device(x=xq if dx else me["x"], z=zq if dz else me["z"])
            quad_copies.append(
                send(stage.at[tx * 2 + tz], quad.at[mine], quad_s.at[n], quad_r.at[n], to)
            )

    def piece():
        need(*quad_copies)
        quad[mine] = stage[mine]
        rows = jnp.concatenate([quad[k, 0:OWN, :].astype(F32) for k in range(4)], axis=0)
        w[kx, kz, me["z"] % 2, me["y"], core, me["x"] // 2] = rows.astype(BF16)

    contract = (((1,), (1,)), ((), ()))

    def at_of(kind, at, r0, n):
        x, y, z, c = at["x"], at["y"], at["z"], at["core"]
        whole = lambda v: isinstance(v, slice)
        zhi, zlo = (ALL, ALL) if whole(z) else (z // 2, z % 2)
        rows = pl.ds(r0, n)
        if kind == "down":
            return dt_raw.at[zlo, y, c, x, zhi, rows, :]
        xhi, xlo = (ALL, ALL) if whole(x) else (x // 2, x % 2)
        return w.at[xlo, zhi, zlo, y, c, xhi, rows, :]

    done = set()

    def need(*copies):
        for copy in copies:
            if id(copy) not in done:
                done.add(id(copy))
                copy.wait_recv()

    class Stream:
        def __init__(self, name, n):
            self.n = n
            self.kind, (self.a, self.b, self.c), self.r0, self.rows = STREAMS[name]
            self.cut = self.rows // 32 * 16
            self.copies = {}
            self.sibs = {}

        def ref(self, at, part=None):
            r0, rows = self.r0, self.rows
            if part == 0:
                rows = self.cut
            elif part == 1:
                r0, rows = r0 + self.cut, rows - self.cut
            return at_of(self.kind, {**me, "core": core, **at}, r0, rows)

        def go(self, key, axis, by, at, part=None):
            ref = self.ref(at, part)
            n = len(self.copies)
            self.copies[key] = send(
                ref, ref, ag_s.at[self.n, n], ag_r.at[self.n, n], device(**{axis: step(axis, by)})
            )

        def sib(self, key, at):
            ref = self.ref(at)
            n = len(self.sibs)
            self.sibs[key] = send(ref, ref, sib_s.at[self.n, n], sib_r.at[self.n, n], sibling)

        def open(self, name, axis, at):
            at = {**at, axis: me[axis]}
            self.go(name + "P", axis, side[axis], at)
            self.go(name + "O", axis, -side[axis], at)

        def onward(self, name, end, axis, at):
            d = side[axis] if end == "P" else -side[axis]
            need(self.copies[name + end])
            key = name + ("o" if end == "P" else "p")
            self.go(key, axis, -d, {**at, axis: step(axis, d)}, 0 if end == "P" else 1)

        def close(self, name):
            need(self.copies[name + "o"], self.copies[name + "p"])

        def sub(self, j):
            d = side[self.b]
            return {self.a: ALL, self.b: step(self.b, (0, d, -d, 2)[j])}

        def open1(self):
            for by in (1, 2, 3):
                self.go(f"1{by}", self.a, by, {})

        def close1(self):
            need(*(self.copies[f"1{by}"] for by in (1, 2, 3)))
            self.open("2", self.b, {self.a: ALL})
            self.sib("20", self.sub(0))

        def fwd2(self, end):
            self.onward("2", end, self.b, {self.a: ALL})
            j = 1 if end == "P" else 2
            self.sib(f"2{j}", self.sub(j))

        def close2(self):
            self.close("2")
            self.sib("23", self.sub(3))

        def open3(self, j):
            self.open(f"3{j}", self.c, self.sub(int(j)))

        def fwd3(self, end, j):
            at = self.sub(int(j))
            self.onward(f"3{j}", end, self.c, at)
            d = side[self.c] if end == "P" else -side[self.c]
            self.sib(f"3{j}{end}", {**at, self.c: step(self.c, d)})

        def close3(self, j):
            self.close(f"3{j}")
            self.sib(f"3{j}o", {**self.sub(int(j)), self.c: step(self.c, 2)})

        def need_sib(self, *keys):
            need(*(self.sibs[key] for key in keys))

        def end(self):
            need(*self.copies.values(), *self.sibs.values())
            for copy in list(self.copies.values()) + list(self.sibs.values()):
                copy.wait_send()

    streams = {name: Stream(name, n) for n, name in enumerate(STREAMS)}

    x0_copies = []
    state = {}

    def raised():
        loads[2].wait()
        loads[3].wait()
        loads[4].wait()
        first = (outer % 2 * 8 + inner) * ROWS
        position = first + lax.broadcasted_iota(jnp.int32, (ROWS, KV), 0)
        live = jnp.where(position < lengths[outer // 2], 1.0, 0.0).astype(BF16)
        masked[...] = cot[...] * live
        back = lax.dot_general(masked[...], up[...], contract, preferred_element_type=F32)
        state["raised2"] = back.astype(BF16) * jnp.asarray(adapter_scale, BF16)
        state["raised2_t"] = state["raised2"].astype(F32).T.astype(BF16)
        total[...] = jnp.zeros_like(total)

    def owners(c):
        loads[5 + c].wait()
        for n in range(0, STEP, 256):
            m = min(256, STEP - n)
            g[:, n : n + m] = jnp.dot(
                state["raised2_t"], tokens[:, STEP * c + n : STEP * c + n + m], preferred_element_type=F32
            )
        for i in range(32):
            o, x, zhi = i // 8, i // 2 % 4, i % 2
            piece = g[:, OWN * i : OWN * (i + 1)]
            r[c // 2, 2 * (c % 2) + o // 2, o % 2, x, zhi, :, 0:OWN] = piece
            r[c // 2, 2 * (c % 2) + o // 2, o % 2, x, zhi, :, OWN:128] = jnp.zeros((RANK, 128 - OWN), F32)

    def owners_pair(c):
        zlo, y = c // 2, pl.ds(2 * (c % 2), 2)
        x0_copies.append(
            send(r.at[zlo, y, 1 - core], x0.at[zlo, y], rs_s.at[0, c], rs_r.at[0, c], sibling)
        )

    def add_sibling(c):
        need(x0_copies[c])
        for y in range(2 * (c % 2), 2 * (c % 2) + 2):
            for x in range(4):
                r[c // 2, y, core, x] = r[c // 2, y, core, x] + x0[c // 2, y, x]

    def r_at(at, r0, n):
        z = at["z"]
        zhi, zlo = (ALL, ALL) if isinstance(z, slice) else (z // 2, z % 2)
        return r.at[zlo, at["y"], core, at["x"], zhi, pl.ds(r0, n), :]

    class Sum:
        def __init__(self, n):
            self.n = n
            (self.a, self.b, self.c), self.r0, self.rows, self.cut = SUMS[n]
            self.free = {self.a: ALL, self.b: ALL, self.c: ALL}
            self.sends = []

        def go(self, src, dst, k, axis, by):
            copy = send(src, dst, rs_s.at[1 + self.n, k], rs_r.at[1 + self.n, k], device(**{axis: step(axis, by)}))
            self.sends.append(copy)
            return copy

        def at(self, by, half=None):
            r0, rows = self.r0, self.rows
            if half == 0:
                rows = self.cut
            elif half == 1:
                r0, rows = r0 + self.cut, rows - self.cut
            return r_at({**self.free, self.a: step(self.a, by)}, r0, rows)

        def pack(self, buffer, ref):
            buffer[...] = ref[...].reshape(buffer.shape).astype(BF16)
            return buffer

        def take(self, ref, buffer):
            ref[...] = ref[...] + buffer[...].astype(F32).reshape(ref.shape)

        def first(self):
            n = self.n
            self.ca = self.go(self.pack(sa[n], self.at(2, 0)), xa[n], 0, self.a, 1)
            self.cb = self.go(self.pack(sb[n], self.at(2, 1)), xb[n], 1, self.a, -1)

        def second(self):
            n = self.n
            need(self.ca)
            self.take(self.at(1, 0), xa[n])
            self.cl = self.go(self.pack(sl[n], self.at(1)), xl[n], 2, self.a, 1)
            need(self.cb)
            self.take(self.at(-1, 1), xb[n])
            self.cr = self.go(self.pack(sr[n], self.at(-1)), xr[n], 3, self.a, -1)

        def third(self):
            need(self.cl, self.cr)
            self.take(self.at(0), xl[self.n])
            self.take(self.at(0), xr[self.n])
            self.k = []
            for j, by in enumerate((1, -1, 2)):
                src = r_at({**self.free, self.a: me[self.a], self.b: step(self.b, by)}, self.r0, self.rows)
                self.k.append(self.go(src, y2[self.n].at[j], 4 + j, self.b, by))

        def fourth(self):
            need(*self.k)
            ref = r_at({**me, self.c: ALL}, self.r0, self.rows)
            ref[...] = ref[...] + y2[self.n][0] + y2[self.n][1] + y2[self.n][2]
            self.k = []
            for j, by in enumerate((1, -1, 2)):
                src = r_at({**me, self.c: step(self.c, by)}, self.r0, self.rows)
                self.k.append(self.go(src, y3[self.n].at[j], 7 + j, self.c, by))

        def fifth(self):
            need(*self.k)
            own = r_at(me, self.r0, self.rows)
            total = own[...] + y3[self.n][0] + y3[self.n][1] + y3[self.n][2]
            dgrad[self.r0 : self.r0 + self.rows, :] = total[:, 0:OWN]

        def end(self):
            for copy in self.sends:
                copy.wait_send()

    sums = [Sum(n) for n in range(3)]

    up_copies = []

    def up_send(src, dst, to):
        k = len(up_copies)
        copy = send(src, dst, up_s.at[k], up_r.at[k], to)
        up_copies.append(copy)
        return copy

    others = [(c, by) for c in range(2) for by in range(4) if (c, by) != (0, 0)]

    def up_rows(c, z):
        return pl.ds(pl.multiple_of(c * 32 + z * 8, 8), 8)

    def low_rows():
        down = streams["D"]
        down.need_sib(*down.sibs)
        for c in range(4):
            for i in range(32):
                o, x, zhi = i // 8, i // 2 % 4, i % 2
                piece = dt_raw[c // 2, 2 * (c % 2) + o // 2, o % 2, x, zhi]
                dt[:, OWN * i + STEP * c : OWN * (i + 1) + STEP * c] = piece[:, 0:OWN]

    def low():
        low = jnp.zeros((ROWS, RANK), F32)
        for c in range(29):
            low += lax.dot_general(
                tokens[:, 512 * c : 512 * (c + 1)], dt[:, 512 * c : 512 * (c + 1)], contract,
                preferred_element_type=F32,
            )
        lowered2 = low.astype(BF16) * jnp.asarray(adapter_scale, BF16)
        lowered2_t = lowered2.astype(F32).T.astype(BF16)
        u0[...] = jnp.dot(lowered2_t, masked[...], preferred_element_type=F32)
        state["k"] = []
        for j, (c, by) in enumerate(others):
            to_core, z = core + c - 2 * c * core, step("z", by)
            state["k"].append(up_send(u0.at[up_rows(to_core, z)], u1.at[j], device(core=to_core, z=z)))
        total[...] += jnp.dot(lowered2, up[...], preferred_element_type=F32)

    def wait_up():
        need(*state["k"])

    def up_x():
        wait_up()
        part = u0[up_rows(core, me["z"]), :]
        for j in range(len(others)):
            part = part + u1[j]
        u2[me["x"]] = part
        ref = u2.at[me["x"]]
        state["k"] = [up_send(ref, ref, device(x=step("x", by))) for by in (1, 2, 3)]

    def up_y():
        wait_up()
        u3[me["y"]] = u2[0] + u2[1] + u2[2] + u2[3]
        ref = u3.at[me["y"]]
        state["k"] = [up_send(ref, ref, device(y=step("y", by))) for by in (1, 2, 3)]

    def up_gather():
        wait_up()
        own = up_rows(core, me["z"])
        ugrad[own, :] = u3[0] + u3[1] + u3[2] + u3[3]
        ref = ugrad.at[own]
        state["k"] = [
            up_send(ref, ref, device(core=core + c - 2 * c * core, z=step("z", by))) for c, by in others
        ]

    w3 = w.reshape(4, D, 128)

    def rows_of(j, zlo):
        d = side["y"]
        y = step("y", (0, d, -d, 2)[j])
        odd, early = y % 2, j % 2 == 0
        start = odd * 1920 if early else odd * 1792
        zlo = (me["z"] + 1 + zlo) % 2
        return zlo * 7424 + (y // 2) * STEP + start, 1792 if early else 1920

    def weights(base, size):
        at = pl.ds(pl.multiple_of(base, 128), size)
        return at, jnp.concatenate([w3[k, at, :] for k in range(4)], axis=1)

    def keys_part(j, zlo):
        streams["X"].need_sib(f"2{j}", *(f"3{j}{end}" for end in "POo"))
        streams["Z"].need_sib(*((f"2{j}", f"3{j}o") if zlo else (f"3{j}P", f"3{j}O")))
        if j == 0:
            streams["Y"].need_sib(*(f"2{i}" for i in range(4)))
        else:
            streams["Y"].need_sib(*(f"3{i}{' POo'[j]}" for i in range(4)))
        at, wc = weights(*rows_of(j, zlo))
        total[...] += jnp.dot(tokens[:, at], wc, preferred_element_type=F32)

    def input_part(j, zlo):
        base, size = rows_of(j, zlo)
        for n in range(0, size, 256):
            at, wc = weights(base + n, min(256, size - n))
            out = lax.dot_general(masked[...], wc, contract, preferred_element_type=F32)
            out += jnp.dot(state["raised2"], dt[:, at], preferred_element_type=F32)
            ig[:, at] = out.astype(BF16)

    def add_siblings():
        for c in range(4):
            add_sibling(c)

    D_, Z_, X_, Y_ = streams.values()
    fill_stage()
    raised()
    owners(0)
    exchange()
    D_.open1()
    piece()
    Z_.open1()
    X_.open1()
    Y_.open1()
    owners(1)
    owners(2)
    owners_pair(0)
    owners_pair(1)
    owners_pair(2)
    owners(3)
    owners_pair(3)
    D_.close1()
    D_.open3(0)
    X_.close1()
    X_.open3(0)
    Z_.close1()
    Z_.open3(0)
    add_siblings()
    sums[0].first()
    D_.fwd2("P")
    D_.fwd2("O")
    D_.fwd3("O", 0)
    D_.open3(1)
    D_.open3(2)
    Y_.close1()
    D_.fwd3("P", 0)
    Y_.open3(0)
    X_.fwd2("P")
    X_.open3(1)
    X_.fwd2("O")
    X_.fwd3("O", 0)
    X_.fwd3("P", 0)
    sums[2].first()
    Z_.fwd3("P", 0)
    Z_.fwd3("O", 0)
    D_.close2()
    D_.fwd3("O", 1)
    D_.fwd3("P", 1)
    D_.open3(3)
    sums[1].first()
    Z_.fwd2("P")
    Z_.open3(1)
    D_.fwd3("O", 2)
    D_.fwd3("P", 2)
    Z_.fwd2("O")
    D_.close3(0)
    Y_.fwd2("P")
    Y_.fwd2("O")
    X_.open3(2)
    Y_.open3(1)
    X_.fwd3("P", 1)
    Y_.fwd3("P", 0)
    Y_.fwd3("O", 0)
    X_.fwd3("O", 1)
    X_.close2()
    Z_.close3(0)
    X_.close3(0)
    Z_.open3(2)
    D_.close3(1)
    D_.fwd3("P", 3)
    D_.fwd3("O", 3)
    X_.open3(3)
    Y_.open3(2)
    D_.close3(2)
    Z_.close2()
    Z_.fwd3("P", 1)
    Z_.fwd3("O", 1)
    X_.fwd3("P", 2)
    Y_.close2()
    Y_.fwd3("O", 1)
    X_.fwd3("O", 2)
    Y_.fwd3("P", 1)
    Z_.open3(3)
    sums[0].second()
    keys_part(0, 0)
    Y_.open3(3)
    D_.close3(3)
    keys_part(0, 1)
    X_.close3(1)
    Y_.close3(0)
    low_rows()
    low()
    sums[1].second()
    sums[2].second()
    Z_.fwd3("P", 2)
    Z_.fwd3("O", 2)
    X_.fwd3("P", 3)
    Y_.fwd3("O", 2)
    X_.fwd3("O", 3)
    sums[0].third()
    Y_.fwd3("P", 2)
    Z_.close3(1)
    X_.close3(2)
    Y_.close3(1)
    input_part(0, 0)
    Y_.fwd3("O", 3)
    Y_.fwd3("P", 3)
    Z_.fwd3("P", 3)
    Z_.fwd3("O", 3)
    input_part(0, 1)
    up_x()
    keys_part(2, 0)
    keys_part(1, 0)
    keys_part(1, 1)
    sums[1].third()
    sums[2].third()
    X_.close3(3)
    input_part(1, 0)
    up_y()
    Z_.close3(2)
    input_part(1, 1)
    sums[0].fourth()
    Y_.close3(2)
    Z_.close3(3)
    keys_part(2, 1)
    Y_.close3(3)
    input_part(2, 0)
    input_part(2, 1)
    up_gather()
    sums[2].fourth()
    sums[1].fourth()
    keys_part(3, 0)
    sums[0].fifth()
    keys_part(3, 1)
    input_part(3, 0)
    input_part(3, 1)
    sums[2].fifth()
    wait_up()
    sums[1].fifth()
    keys[...] = total[...].astype(BF16)
    for s in streams.values():
        s.end()
    for s in sums:
        s.end()
    for copy in quad_copies + x0_copies + up_copies:
        copy.wait_send()


PARTS = 8


def store_kernel(ig, keys, dgrad, ugrad, ig_hbm, keys_hbm, dgrad_hbm, ugrad_hbm, sem):
    rows = [pl.ds(n * (ROWS // PARTS), ROWS // PARTS) for n in range(PARTS)]
    pairs = [(ig.at[at], ig_hbm.at[at]) for at in rows]
    pairs += [(keys, keys_hbm), (dgrad, dgrad_hbm), (ugrad, ugrad_hbm)]
    copies = [pltpu.make_async_copy(a, b, sem.at[n]) for n, (a, b) in enumerate(pairs)]
    for copy in copies:
        copy.start()
    for copy in copies:
        copy.wait()


def on_device(tokens, cotangent, lengths, frozen, down_weight, up_weight):
    vmem = pl.BlockSpec(memory_space=pltpu.VMEM)
    anywhere = pl.BlockSpec(memory_space=pl.ANY)
    in_hbm = lambda array: pltpu.with_memory_space_constraint(array, pltpu.HBM)
    down_t = down_weight.T
    def halves(rows):
        return [pltpu.VMEM((16 * rows(n), 128), BF16) for n in range(3)]

    def buffers(shape):
        return [pltpu.VMEM(shape(n), F32) for n in range(3)]

    def cdims(axis):
        return (2, 2) if axis == "z" else (4,)

    scratch = [
        pltpu.VMEM((2, 2, 2, 4, 2, 2, QUAD, 128), BF16),
        pltpu.VMEM((RANK, D), BF16),
        pltpu.VMEM((ROWS, D), BF16),
        pltpu.SMEM((8,), jnp.int32),
        pltpu.VMEM((ROWS, KV), BF16),
        pltpu.VMEM((OWN, KV), BF16),
        pltpu.VMEM((RANK, OWN), BF16),
        pltpu.VMEM((RANK, KV), BF16),
        pltpu.VMEM((ROWS, KV), BF16),
        pltpu.VMEM((ROWS, KV), F32),
        pltpu.VMEM((4, 128, 128), BF16),
        pltpu.VMEM((4, 128, 128), BF16),
        pltpu.VMEM((2, 4, 2, 4, 2, RANK, 128), BF16),
        pltpu.VMEM((RANK, STEP), F32),
        pltpu.VMEM((2, 4, 2, 4, 2, RANK, 128), F32),
        pltpu.VMEM((2, 4, 4, 2, RANK, 128), F32),
        *[halves(lambda n: SUMS[n][3]), halves(lambda n: SUMS[n][2] - SUMS[n][3])],
        *[halves(lambda n: SUMS[n][2]) for _ in range(2)],
        *[halves(lambda n: SUMS[n][3]), halves(lambda n: SUMS[n][2] - SUMS[n][3])],
        *[halves(lambda n: SUMS[n][2]) for _ in range(2)],
        buffers(lambda n: (3,) + cdims(SUMS[n][0][2]) + (SUMS[n][2], 128)),
        buffers(lambda n: (3, SUMS[n][2], 128)),
        pltpu.VMEM((RANK, KV), F32),
        pltpu.VMEM((7, 8, KV), F32),
        pltpu.VMEM((4, 8, KV), F32),
        pltpu.VMEM((4, 8, KV), F32),
        pltpu.SemaphoreType.DMA((9,)),
        pltpu.SemaphoreType.DMA((3,)),
        pltpu.SemaphoreType.DMA((3,)),
        pltpu.SemaphoreType.DMA((4, 24)),
        pltpu.SemaphoreType.DMA((4, 24)),
        pltpu.SemaphoreType.DMA((4, 16)),
        pltpu.SemaphoreType.DMA((4, 16)),
        pltpu.SemaphoreType.DMA((4, 10)),
        pltpu.SemaphoreType.DMA((4, 10)),
        pltpu.SemaphoreType.DMA((20,)),
        pltpu.SemaphoreType.DMA((20,)),
    ]
    shapes = (((ROWS, D), BF16), ((ROWS, KV), BF16), ((RANK, OWN), F32), ((RANK, KV), F32))
    inputs = (lengths, tokens, cotangent, frozen, down_t, up_weight)
    results = pl.pallas_call(
        comm_kernel,
        out_shape=tuple(pltpu.VMEM(*shape) for shape in shapes),
        in_specs=[anywhere] * 6,
        out_specs=(vmem,) * 4,
        scratch_shapes=scratch,
        compiler_params=pltpu.CompilerParams(
            collective_id=0, has_side_effects=True, vmem_limit_bytes=46 * 1024 * 1024
        ),
        name="gather_multiply_sum",
    )(*[in_hbm(array) for array in inputs])
    results = [pltpu.with_memory_space_constraint(array, pltpu.VMEM) for array in results]
    ig, keys, dgrad, ugrad = pl.pallas_call(
        store_kernel,
        out_shape=tuple(jax.ShapeDtypeStruct(*shape) for shape in shapes),
        in_specs=[vmem] * 4,
        out_specs=(anywhere,) * 4,
        scratch_shapes=[pltpu.SemaphoreType.DMA((PARTS + 3,))],
        compiler_params=pltpu.CompilerParams(vmem_limit_bytes=4 * 1024 * 1024),
        name="store",
    )(*results)
    return keys, ig, dgrad.T, ugrad


def solution(mesh):
    return jax.shard_map(
        on_device,
        mesh=mesh,
        in_specs=(
            P(("outer", "inner"), None),
            P(("outer", "inner"), None),
            P(),
            P(("outer", "inner"), None),
            P(("outer", "inner"), None),
            P(),
        ),
        out_specs=(
            P(("outer", "inner"), None),
            P(("outer", "inner"), None),
            P(("outer", "inner"), None),
            P(),
        ),
        check_vma=False,
    )
```

time: 877 us -> 69.3 us (0.08)
  waiting for transfers between devices: 776 us -> 0 us
  Pallas kernels: 0 us -> 68.3 us
  matrix products: 52.9 us -> 0 us
  local copies, waits for them, and re-layouts: 31.6 us -> 0 us
  between operations: 13.8 us -> 0.8 us
    all_gather x2 -> x0, waiting for transfers between devices: 622 us -> none  [the longest x1 324 us: on_device(): lax.all_gather(frozen, ('outer', 'inner'), axis=0, tiled=True)]
    psum x1 -> x0, waiting for transfers between devices: 153 us -> none  [on_device(): lax.psum((down_product, up_product), ('outer', 'inner'))]
    pallas_call x0 -> x2, Pallas kernels: none -> 68.3 us  [the longest x1 65.1 us: on_device(): pl.pallas_call(comm_kernel, out_shape=tuple((pltpu.VMEM(*shape) for shape...]
    dot_general x8 -> x0, matrix products: 52.9 us -> none  [the longest x1 18.5 us: on_device(): lax.dot_general(masked_tokens, back_w, contract_product, preferred_elemen...]
    unnamed x15 -> x0, local copies, waits for them, and re-layouts: 25.8 us -> none
  transfers between devices with their start and end apart: 3 -> 0, of which waited for: 3 -> 0; matrix products, arithmetic and copies ran while one was open for 1% -> 0% of each run, Pallas kernels for 0% -> 0%
where the time goes in v2:
time: 69.3 us; the launch traced here: 69.1 us
  Pallas kernels  68.3 us (99%)
  between operations  0.8 us (1%)
    pallas_call x1, Pallas kernels, on_device(): pl.pallas_call(comm_kernel, out_shape=tuple((pltpu.VMEM(*shape) for shape...  65.1 us
    pallas_call x1, Pallas kernels, on_device(): pl.pallas_call(store_kernel, out_shape=tuple((jax.ShapeDtypeStruct(*shape...  3.26 us

profile of v2, /device:TPU:1, one launch (start us, length us, event | category | flops | bytes accessed | tf_op | source)
XLA Modules:
  0.0 69.1 jit_solution(13058515507171377062)
XLA Ops:
  0.6 65.1 %gather_multiply_sum.1 = (bf16[256,14848]{1,0:T(8,128)(2,1)S(1)}, bf16[256,512]{1,0:T(8,128)(2,1)S(1)}, f32[64,116]{1,0:T(8,128)S(1)}, f32[64,512]{1,0:T(8,128)S(1)}) custom-call(s32[8]{0:T(128)} %lengths_hbm.1, bf16[256,14848]{1,0:T(8,128)(2,1)} %tokens_hbm.1, bf16[256,512]{1,0:T(8,128)(2,1)} %cot_hbm.1, bf16[116,512]{1,0:T(8,128)(2,1)} %frozen_hbm.1, ...), custom_call_target="tpu_custom_call" | custom-call | tf_op jit(solution)/shard_map/gather_multiply_sum/pallas_call | solution.py:638
  65.7 3.3 %store.1 = (bf16[256,14848]{1,0:T(8,128)(2,1)}, bf16[256,512]{1,0:T(8,128)(2,1)}, f32[64,116]{1,0:T(8,128)}, f32[64,512]{1,0:T(8,128)}) custom-call(bf16[256,14848]{1,0:T(8,128)(2,1)S(1)} %get-tuple-element.12.ig, bf16[256,512]{1,0:T(8,128)(2,1)S(1)} %get-tuple-element.13.keys, f32[64,116]{1,0:T(8,128)S(1)} %get-tuple-element.14.dgrad, ...), custom_call_target="tpu_custom_call" | custom-call | tf_op jit(solution)/shard_map/store/pallas_call | solution.py:650

commit v3 on v2

--- a/solution.py
+++ b/solution.py
@@ -12,27 +12,56 @@
 QUAD = 4 * OWN
 STEP = 3712
 adapter_scale = 2.0
+BEHIND = 90
 
 STREAMS = {
-    "D": ("down", "yzx", 0, 64),
-    "Z": ("w", "xyz", 0, 192),
-    "X": ("w", "zyx", 192, 128),
-    "Y": ("w", "xzy", 320, 144),
+    "D": ("down", "yxz", 0, 64),
+    "Z": ("w", "xyz", 0, 160),
+    "X": ("w", "zyx", 160, 176),
+    "Y": ("w", "zxy", 336, 128),
 }
 SUMS = (("xyz", 0, 24, 8), ("yzx", 24, 24, 16), ("zxy", 48, 16, 8))
 ALL = slice(None)
 
 
+CONTRACT = (((1,), (1,)), ((), ()))
+
+
+def place(outer, inner):
+    return {"x": inner // 2, "y": (outer // 2) % 4, "z": (inner % 2) * 2 + outer // 8}
+
+
+def rows_of(me, j, own):
+    d = 1 - 2 * (me["y"] % 2)
+    y = (me["y"] + (0, d, -d, 2)[j] + 4) % 4
+    odd, early = y % 2, j % 2 == 0
+    start = odd * 1920 if early else odd * 1792
+    zlo = (me["z"] + 1 + own) % 2
+    return zlo * 7424 + (y // 2) * STEP + start, 1792 if early else 1920
+
+
+def weights(w3, base, size):
+    at = pl.ds(pl.multiple_of(base, 128), size)
+    return at, jnp.concatenate([w3[k, at, :] for k in range(4)], axis=1)
+
+
+def input_columns(w3, dt, masked, raised2, base, size):
+    at, wc = weights(w3, base, size)
+    out = lax.dot_general(masked[...], wc, CONTRACT, preferred_element_type=F32)
+    out += jnp.dot(raised2, dt[:, at], preferred_element_type=F32)
+    return out.astype(BF16)
+
+
 def comm_kernel(
     lengths_hbm, tokens_hbm, cot_hbm, frozen_hbm, down_hbm, up_hbm,
-    ig, keys, dgrad, ugrad,
-    w, dt, tokens, lengths, cot, frozen, down_t, up, masked, total,
-    stage, quad, dt_raw, g, r, x0, sa, sb, sl, sr, xa, xb, xl, xr, y2, y3, u0, u1, u2, u3,
+    ig, total, dgrad, ugrad, w_last, dt_last, tokens_last, masked, raised_out,
+    w, dt, tokens, lengths, cot, frozen, down_t, up,
+    stage, quad, dt_raw, g, r, x0, sa, sb, sl, sr, sy, xa, xb, xl, xr, y2, y3, u0, u1, u2, u3,
     load_sem, quad_s, quad_r, ag_s, ag_r, sib_s, sib_r, rs_s, rs_r, up_s, up_r,
 ):
     outer, inner = lax.axis_index("outer"), lax.axis_index("inner")
     core = outer % 2
-    me = {"x": inner // 2, "y": (outer // 2) % 4, "z": (inner % 2) * 2 + outer // 8}
+    me = place(outer, inner)
     side = {a: 1 - 2 * (me[a] % 2) for a in "xyz"}
 
     def device(core=core, **at):
@@ -49,7 +78,19 @@
             src_ref=src, dst_ref=dst, send_sem=s, recv_sem=r_, device_id=to, device_id_type=MESH
         )
         copy.start()
+        sent.append(copy)
+        if len(sent) > BEHIND:
+            left(sent[len(sent) - 1 - BEHIND])
         return copy
+
+    gone = set()
+
+    def left(copy):
+        if id(copy) not in gone:
+            gone.add(id(copy))
+            copy.wait_send()
+
+    sent = []
 
     barrier = pltpu.get_barrier_semaphore()
     peers = [device(**{a: step(a, by)}) for a in "xyz" for by in (1, 2, 3)]
@@ -82,8 +123,10 @@
         loads[1].wait()
         dt_raw[at_home] = jnp.concatenate([down_t[...], jnp.zeros((RANK, 128 - OWN), BF16)], axis=1)
 
+    def enter():
+        pl.semaphore_wait(barrier, len(peers))
+
     def exchange():
-        pl.semaphore_wait(barrier, len(peers))
         for n, (dx, dz) in enumerate(((1, 0), (0, 1), (1, 1))):
             tx, tz = (kx + dx) % 2, (kz + dz) % 2
             to = device(x=xq if dx else me["x"], z=zq if dz else me["z"])
@@ -96,8 +139,6 @@
         quad[mine] = stage[mine]
         rows = jnp.concatenate([quad[k, 0:OWN, :].astype(F32) for k in range(4)], axis=0)
         w[kx, kz, me["z"] % 2, me["y"], core, me["x"] // 2] = rows.astype(BF16)
-
-    contract = (((1,), (1,)), ((), ()))
 
     def at_of(kind, at, r0, n):
         x, y, z, c = at["x"], at["y"], at["z"], at["core"]
@@ -122,6 +163,7 @@
             self.n = n
             self.kind, (self.a, self.b, self.c), self.r0, self.rows = STREAMS[name]
             self.cut = self.rows // 32 * 16
+            self.direct = name == "D"
             self.copies = {}
             self.sibs = {}
 
@@ -145,14 +187,19 @@
             n = len(self.sibs)
             self.sibs[key] = send(ref, ref, sib_s.at[self.n, n], sib_r.at[self.n, n], sibling)
 
-        def open(self, name, axis, at):
+        def both(self, name, axis, at, k=""):
             at = {**at, axis: me[axis]}
-            self.go(name + "P", axis, side[axis], at)
-            self.go(name + "O", axis, -side[axis], at)
+            for end, by in (("P", side[axis]), ("O", -side[axis])):
+                self.go(name + end + k, axis, by, at)
+
+        def need_all(self, start):
+            need(*(copy for key, copy in self.copies.items() if key[: len(start)] == start))
 
         def onward(self, name, end, axis, at):
             d = side[axis] if end == "P" else -side[axis]
-            need(self.copies[name + end])
+            self.need_all(name + end)
+            if self.direct and name == "2":
+                return
             key = name + ("o" if end == "P" else "p")
             self.go(key, axis, -d, {**at, axis: step(axis, d)}, 0 if end == "P" else 1)
 
@@ -164,12 +211,23 @@
             return {self.a: ALL, self.b: step(self.b, (0, d, -d, 2)[j])}
 
         def open1(self):
-            for by in (1, 2, 3):
-                self.go(f"1{by}", self.a, by, {})
+            for k in (1, 2, 3):
+                self.go(f"1{k}", self.a, k, {})
+
+        def row(self, k):
+            if k:
+                need(self.copies[f"1{k}"])
+            return {self.a: step(self.a, -k)}
+
+        def open2(self, k):
+            self.both("2", self.b, self.row(k), str(k))
+            if self.direct:
+                self.go(f"2X{k}", self.b, 2, self.row(k))
+
+        def open30(self, k):
+            self.both("30", self.c, self.row(k), str(k))
 
         def close1(self):
-            need(*(self.copies[f"1{by}"] for by in (1, 2, 3)))
-            self.open("2", self.b, {self.a: ALL})
             self.sib("20", self.sub(0))
 
         def fwd2(self, end):
@@ -178,33 +236,31 @@
             self.sib(f"2{j}", self.sub(j))
 
         def close2(self):
-            self.close("2")
+            if self.direct:
+                self.need_all("2X")
+            else:
+                self.close("2")
             self.sib("23", self.sub(3))
 
         def open3(self, j):
-            self.open(f"3{j}", self.c, self.sub(int(j)))
+            self.both(f"3{j}", self.c, self.sub(j))
 
         def fwd3(self, end, j):
-            at = self.sub(int(j))
+            at = self.sub(j)
             self.onward(f"3{j}", end, self.c, at)
             d = side[self.c] if end == "P" else -side[self.c]
             self.sib(f"3{j}{end}", {**at, self.c: step(self.c, d)})
 
         def close3(self, j):
             self.close(f"3{j}")
-            self.sib(f"3{j}o", {**self.sub(int(j)), self.c: step(self.c, 2)})
+            self.sib(f"3{j}o", {**self.sub(j), self.c: step(self.c, 2)})
 
         def need_sib(self, *keys):
             need(*(self.sibs[key] for key in keys))
 
-        def end(self):
-            need(*self.copies.values(), *self.sibs.values())
-            for copy in list(self.copies.values()) + list(self.sibs.values()):
-                copy.wait_send()
-
     streams = {name: Stream(name, n) for n, name in enumerate(STREAMS)}
 
-    x0_copies = []
+    x0_copies = {}
     state = {}
 
     def raised():
@@ -215,8 +271,9 @@
         position = first + lax.broadcasted_iota(jnp.int32, (ROWS, KV), 0)
         live = jnp.where(position < lengths[outer // 2], 1.0, 0.0).astype(BF16)
         masked[...] = cot[...] * live
-        back = lax.dot_general(masked[...], up[...], contract, preferred_element_type=F32)
+        back = lax.dot_general(masked[...], up[...], CONTRACT, preferred_element_type=F32)
         state["raised2"] = back.astype(BF16) * jnp.asarray(adapter_scale, BF16)
+        raised_out[...] = state["raised2"]
         state["raised2_t"] = state["raised2"].astype(F32).T.astype(BF16)
         total[...] = jnp.zeros_like(total)
 
@@ -235,9 +292,7 @@
 
     def owners_pair(c):
         zlo, y = c // 2, pl.ds(2 * (c % 2), 2)
-        x0_copies.append(
-            send(r.at[zlo, y, 1 - core], x0.at[zlo, y], rs_s.at[0, c], rs_r.at[0, c], sibling)
-        )
+        x0_copies[c] = send(r.at[zlo, y, 1 - core], x0.at[zlo, y], rs_s.at[0, c], rs_r.at[0, c], sibling)
 
     def add_sibling(c):
         need(x0_copies[c])
@@ -298,12 +353,14 @@
             self.k = []
             for j, by in enumerate((1, -1, 2)):
                 src = r_at({**self.free, self.a: me[self.a], self.b: step(self.b, by)}, self.r0, self.rows)
-                self.k.append(self.go(src, y2[self.n].at[j], 4 + j, self.b, by))
+                out = self.pack(sy[self.n].at[j], src)
+                self.k.append(self.go(out, y2[self.n].at[j], 4 + j, self.b, by))
 
         def fourth(self):
             need(*self.k)
             ref = r_at({**me, self.c: ALL}, self.r0, self.rows)
-            ref[...] = ref[...] + y2[self.n][0] + y2[self.n][1] + y2[self.n][2]
+            for j in range(3):
+                self.take(ref, y2[self.n].at[j])
             self.k = []
             for j, by in enumerate((1, -1, 2)):
                 src = r_at({**me, self.c: step(self.c, by)}, self.r0, self.rows)
@@ -314,10 +371,6 @@
             own = r_at(me, self.r0, self.rows)
             total = own[...] + y3[self.n][0] + y3[self.n][1] + y3[self.n][2]
             dgrad[self.r0 : self.r0 + self.rows, :] = total[:, 0:OWN]
-
-        def end(self):
-            for copy in self.sends:
-                copy.wait_send()
 
     sums = [Sum(n) for n in range(3)]
 
@@ -344,10 +397,14 @@
                 dt[:, OWN * i + STEP * c : OWN * (i + 1) + STEP * c] = piece[:, 0:OWN]
 
     def low():
+        base, size = rows_of(me, 3, 1)
+        at = pl.ds(pl.multiple_of(base, 128), size)
+        dt_last[...] = dt[:, at]
+        tokens_last[...] = tokens[:, at]
         low = jnp.zeros((ROWS, RANK), F32)
         for c in range(29):
             low += lax.dot_general(
-                tokens[:, 512 * c : 512 * (c + 1)], dt[:, 512 * c : 512 * (c + 1)], contract,
+                tokens[:, 512 * c : 512 * (c + 1)], dt[:, 512 * c : 512 * (c + 1)], CONTRACT,
                 preferred_element_type=F32,
             )
         lowered2 = low.astype(BF16) * jnp.asarray(adapter_scale, BF16)
@@ -388,35 +445,29 @@
 
     w3 = w.reshape(4, D, 128)
 
-    def rows_of(j, zlo):
-        d = side["y"]
-        y = step("y", (0, d, -d, 2)[j])
-        odd, early = y % 2, j % 2 == 0
-        start = odd * 1920 if early else odd * 1792
-        zlo = (me["z"] + 1 + zlo) % 2
-        return zlo * 7424 + (y // 2) * STEP + start, 1792 if early else 1920
-
-    def weights(base, size):
-        at = pl.ds(pl.multiple_of(base, 128), size)
-        return at, jnp.concatenate([w3[k, at, :] for k in range(4)], axis=1)
-
-    def keys_part(j, zlo):
+    def arrived(j, zlo):
         streams["X"].need_sib(f"2{j}", *(f"3{j}{end}" for end in "POo"))
         streams["Z"].need_sib(*((f"2{j}", f"3{j}o") if zlo else (f"3{j}P", f"3{j}O")))
-        if j == 0:
-            streams["Y"].need_sib(*(f"2{i}" for i in range(4)))
-        else:
-            streams["Y"].need_sib(*(f"3{i}{' POo'[j]}" for i in range(4)))
-        at, wc = weights(*rows_of(j, zlo))
+        subs = ((0, 3) if zlo else (1, 2)) if streams["Y"].b == "z" else range(4)
+        streams["Y"].need_sib(*(f"3{i}{' POo'[j]}" if j else f"2{i}" for i in subs))
+
+    def keys_part(j, zlo):
+        arrived(j, zlo)
+        at, wc = weights(w3, *rows_of(me, j, zlo))
         total[...] += jnp.dot(tokens[:, at], wc, preferred_element_type=F32)
 
+    def last_rows():
+        arrived(3, 1)
+        at, _ = weights(w3, *rows_of(me, 3, 1))
+        w_last[...] = w3[:, at, :]
+
     def input_part(j, zlo):
-        base, size = rows_of(j, zlo)
+        base, size = rows_of(me, j, zlo)
         for n in range(0, size, 256):
-            at, wc = weights(base + n, min(256, size - n))
-            out = lax.dot_general(masked[...], wc, contract, preferred_element_type=F32)
-            out += jnp.dot(state["raised2"], dt[:, at], preferred_element_type=F32)
-            ig[:, at] = out.astype(BF16)
+            m = min(256, size - n)
+            ig[:, pl.ds(pl.multiple_of(base + n, 128), m)] = input_columns(
+                w3, dt, masked, state["raised2"], base + n, m
+            )
 
     def add_siblings():
         for c in range(4):
@@ -426,156 +477,204 @@
     fill_stage()
     raised()
     owners(0)
+    enter()
+    owners_pair(0)
+    D_.open1()
     exchange()
-    D_.open1()
+    owners(2)
+    owners(3)
+    owners_pair(3)
+    D_.open2(0)
+    owners_pair(2)
+    owners(1)
+    owners_pair(1)
+    D_.open30(2)
+    D_.open2(1)
+    D_.open30(1)
+    D_.open2(2)
+    D_.open30(0)
+    D_.open30(3)
+    D_.open2(3)
+    D_.close1()
     piece()
     Z_.open1()
+    Z_.open2(0)
+    Y_.open1()
+    Y_.open2(0)
+    Y_.open30(0)
     X_.open1()
-    Y_.open1()
-    owners(1)
-    owners(2)
-    owners_pair(0)
-    owners_pair(1)
-    owners_pair(2)
-    owners(3)
-    owners_pair(3)
-    D_.close1()
-    D_.open3(0)
-    X_.close1()
-    X_.open3(0)
-    Z_.close1()
-    Z_.open3(0)
+    X_.open2(0)
     add_siblings()
-    sums[0].first()
+    sums[1].first()
+    X_.open30(0)
+    D_.fwd3("P", 0)
+    D_.fwd3("O", 0)
     D_.fwd2("P")
     D_.fwd2("O")
-    D_.fwd3("O", 0)
+    D_.open3(2)
     D_.open3(1)
-    D_.open3(2)
+    sums[0].first()
+    Y_.open2(1)
+    Y_.open30(1)
+    Y_.open2(2)
+    D_.close2()
+    D_.open3(3)
+    Y_.open30(2)
+    Z_.open2(1)
+    Z_.open2(2)
+    Y_.open2(3)
     Y_.close1()
-    D_.fwd3("P", 0)
-    Y_.open3(0)
+    X_.open2(1)
+    X_.open2(2)
+    Z_.open2(3)
+    Z_.close1()
+    X_.open30(1)
+    X_.open2(3)
+    X_.close1()
+    D_.close3(0)
+    X_.open30(3)
+    sums[2].first()
+    Z_.open30(2)
+    D_.fwd3("P", 2)
+    D_.fwd3("O", 2)
+    X_.open30(2)
+    sums[0].second()
+    Y_.fwd2("P")
+    Z_.open30(1)
+    D_.fwd3("O", 1)
+    D_.fwd3("P", 1)
+    Y_.open30(3)
+    Y_.fwd2("O")
+    Y_.open3(1)
+    D_.fwd3("P", 3)
+    D_.fwd3("O", 3)
+    sums[2].second()
+    X_.fwd3("P", 0)
+    Z_.fwd2("O")
+    Z_.fwd2("P")
+    X_.fwd3("O", 0)
+    X_.fwd2("O")
+    D_.close3(2)
+    Z_.open30(3)
     X_.fwd2("P")
+    Y_.fwd3("O", 0)
+    Z_.open30(0)
+    Y_.fwd3("P", 0)
     X_.open3(1)
-    X_.fwd2("O")
-    X_.fwd3("O", 0)
-    X_.fwd3("P", 0)
-    sums[2].first()
+    D_.close3(1)
+    sums[0].third()
+    Z_.open3(1)
+    D_.close3(3)
+    Y_.close2()
+    Y_.fwd3("O", 1)
+    low_rows()
+    X_.close3(0)
+    Y_.fwd3("P", 1)
+    X_.open3(2)
+    sums[2].third()
     Z_.fwd3("P", 0)
     Z_.fwd3("O", 0)
-    D_.close2()
-    D_.fwd3("O", 1)
-    D_.fwd3("P", 1)
-    D_.open3(3)
-    sums[1].first()
-    Z_.fwd2("P")
-    Z_.open3(1)
-    D_.fwd3("O", 2)
-    D_.fwd3("P", 2)
-    Z_.fwd2("O")
-    D_.close3(0)
-    Y_.fwd2("P")
-    Y_.fwd2("O")
-    X_.open3(2)
-    Y_.open3(1)
+    low()
     X_.fwd3("P", 1)
-    Y_.fwd3("P", 0)
-    Y_.fwd3("O", 0)
+    X_.close2()
+    Y_.open3(2)
+    Z_.open3(2)
+    Z_.close2()
+    keys_part(0, 0)
     X_.fwd3("O", 1)
-    X_.close2()
-    Z_.close3(0)
-    X_.close3(0)
-    Z_.open3(2)
-    D_.close3(1)
-    D_.fwd3("P", 3)
-    D_.fwd3("O", 3)
-    X_.open3(3)
-    Y_.open3(2)
-    D_.close3(2)
-    Z_.close2()
     Z_.fwd3("P", 1)
     Z_.fwd3("O", 1)
+    input_part(0, 0)
+    Y_.open3(3)
+    sums[0].fourth()
+    Z_.close3(0)
+    Y_.close3(0)
+    Y_.close3(1)
+    X_.open3(3)
+    up_x()
     X_.fwd3("P", 2)
-    Y_.close2()
-    Y_.fwd3("O", 1)
+    keys_part(0, 1)
     X_.fwd3("O", 2)
-    Y_.fwd3("P", 1)
+    sums[1].second()
+    input_part(0, 1)
+    Y_.fwd3("O", 2)
+    Y_.fwd3("P", 2)
     Z_.open3(3)
-    sums[0].second()
-    keys_part(0, 0)
-    Y_.open3(3)
-    D_.close3(3)
-    keys_part(0, 1)
+    sums[2].fourth()
+    Z_.fwd3("O", 2)
+    Z_.fwd3("P", 2)
     X_.close3(1)
-    Y_.close3(0)
-    low_rows()
-    low()
-    sums[1].second()
-    sums[2].second()
-    Z_.fwd3("P", 2)
-    Z_.fwd3("O", 2)
-    X_.fwd3("P", 3)
-    Y_.fwd3("O", 2)
-    X_.fwd3("O", 3)
-    sums[0].third()
-    Y_.fwd3("P", 2)
-    Z_.close3(1)
-    X_.close3(2)
-    Y_.close3(1)
-    input_part(0, 0)
     Y_.fwd3("O", 3)
     Y_.fwd3("P", 3)
-    Z_.fwd3("P", 3)
-    Z_.fwd3("O", 3)
-    input_part(0, 1)
-    up_x()
-    keys_part(2, 0)
+    Z_.close3(1)
+    sums[0].fifth()
     keys_part(1, 0)
-    keys_part(1, 1)
     sums[1].third()
-    sums[2].third()
-    X_.close3(3)
+    X_.fwd3("P", 3)
+    X_.fwd3("O", 3)
     input_part(1, 0)
     up_y()
+    keys_part(1, 1)
+    sums[2].fifth()
+    Z_.fwd3("P", 3)
+    X_.close3(2)
+    Z_.fwd3("O", 3)
+    input_part(1, 1)
     Z_.close3(2)
-    input_part(1, 1)
-    sums[0].fourth()
     Y_.close3(2)
+    Y_.close3(3)
+    keys_part(2, 0)
+    input_part(2, 0)
+    X_.close3(3)
+    sums[1].fourth()
+    up_gather()
+    keys_part(2, 1)
+    input_part(2, 1)
     Z_.close3(3)
-    keys_part(2, 1)
-    Y_.close3(3)
-    input_part(2, 0)
-    input_part(2, 1)
-    up_gather()
-    sums[2].fourth()
-    sums[1].fourth()
     keys_part(3, 0)
-    sums[0].fifth()
-    keys_part(3, 1)
     input_part(3, 0)
-    input_part(3, 1)
-    sums[2].fifth()
+    last_rows()
+    sums[1].fifth()
     wait_up()
-    sums[1].fifth()
-    keys[...] = total[...].astype(BF16)
     for s in streams.values():
-        s.end()
-    for s in sums:
-        s.end()
-    for copy in quad_copies + x0_copies + up_copies:
-        copy.wait_send()
-
-
-PARTS = 8
-
-
-def store_kernel(ig, keys, dgrad, ugrad, ig_hbm, keys_hbm, dgrad_hbm, ugrad_hbm, sem):
-    rows = [pl.ds(n * (ROWS // PARTS), ROWS // PARTS) for n in range(PARTS)]
-    pairs = [(ig.at[at], ig_hbm.at[at]) for at in rows]
-    pairs += [(keys, keys_hbm), (dgrad, dgrad_hbm), (ugrad, ugrad_hbm)]
-    copies = [pltpu.make_async_copy(a, b, sem.at[n]) for n, (a, b) in enumerate(pairs)]
-    for copy in copies:
-        copy.start()
+        need(*s.copies.values(), *s.sibs.values())
+    for copy in sent:
+        left(copy)
+
+
+def last_kernel(
+    ig, total, dgrad, ugrad, w, dt, tokens, masked, raised2,
+    keys_hbm, ig_hbm, dgrad_hbm, ugrad_hbm,
+    last, keys, sem,
+):
+    outer, inner = lax.axis_index("outer"), lax.axis_index("inner")
+    me = place(outer, inner)
+    copies = []
+
+    def store(src, dst):
+        copies.append(pltpu.make_async_copy(src, dst, sem.at[len(copies)]))
+        copies[-1].start()
+
+    zlo, pair = me["z"] % 2, me["y"] // 2
+    early, early_size = rows_of(me, 2, 1)
+    for base, size in (
+        ((1 - zlo) * 7424, 7424), (zlo * 7424 + pair * STEP, STEP), (early, early_size)
+    ):
+        at = pl.ds(pl.multiple_of(base, 128), size)
+        store(ig.at[:, at], ig_hbm.at[:, at])
+    store(dgrad, dgrad_hbm)
+    store(ugrad, ugrad_hbm)
+    base, size = rows_of(me, 3, 1)
+    for n in range(0, size, 640):
+        for k in range(n, n + 640, 256):
+            m = min(256, n + 640 - k)
+            last[:, k : k + m] = input_columns(w, dt, masked, raised2[...], k, m)
+        at = pl.ds(pl.multiple_of(base + n, 128), 640)
+        store(last.at[:, n : n + 640], ig_hbm.at[:, at])
+    _, wc = weights(w, 0, size)
+    out = total[...] + jnp.dot(tokens[...], wc, preferred_element_type=F32)
+    keys[...] = out.astype(BF16)
+    store(keys, keys_hbm)
     for copy in copies:
         copy.wait()
 
@@ -588,11 +687,11 @@
     def halves(rows):
         return [pltpu.VMEM((16 * rows(n), 128), BF16) for n in range(3)]
 
+    def fours():
+        return [pltpu.VMEM((3, 4 * SUMS[n][2], 128), BF16) for n in range(3)]
+
     def buffers(shape):
         return [pltpu.VMEM(shape(n), F32) for n in range(3)]
-
-    def cdims(axis):
-        return (2, 2) if axis == "z" else (4,)
 
     scratch = [
         pltpu.VMEM((2, 2, 2, 4, 2, 2, QUAD, 128), BF16),
@@ -603,8 +702,6 @@
         pltpu.VMEM((OWN, KV), BF16),
         pltpu.VMEM((RANK, OWN), BF16),
         pltpu.VMEM((RANK, KV), BF16),
-        pltpu.VMEM((ROWS, KV), BF16),
-        pltpu.VMEM((ROWS, KV), F32),
         pltpu.VMEM((4, 128, 128), BF16),
         pltpu.VMEM((4, 128, 128), BF16),
         pltpu.VMEM((2, 4, 2, 4, 2, RANK, 128), BF16),
@@ -613,9 +710,10 @@
         pltpu.VMEM((2, 4, 4, 2, RANK, 128), F32),
         *[halves(lambda n: SUMS[n][3]), halves(lambda n: SUMS[n][2] - SUMS[n][3])],
         *[halves(lambda n: SUMS[n][2]) for _ in range(2)],
+        fours(),
         *[halves(lambda n: SUMS[n][3]), halves(lambda n: SUMS[n][2] - SUMS[n][3])],
         *[halves(lambda n: SUMS[n][2]) for _ in range(2)],
-        buffers(lambda n: (3,) + cdims(SUMS[n][0][2]) + (SUMS[n][2], 128)),
+        fours(),
         buffers(lambda n: (3, SUMS[n][2], 128)),
         pltpu.VMEM((RANK, KV), F32),
         pltpu.VMEM((7, 8, KV), F32),
@@ -624,8 +722,8 @@
         pltpu.SemaphoreType.DMA((9,)),
         pltpu.SemaphoreType.DMA((3,)),
         pltpu.SemaphoreType.DMA((3,)),
-        pltpu.SemaphoreType.DMA((4, 24)),
-        pltpu.SemaphoreType.DMA((4, 24)),
+        pltpu.SemaphoreType.DMA((4, 40)),
+        pltpu.SemaphoreType.DMA((4, 40)),
         pltpu.SemaphoreType.DMA((4, 16)),
         pltpu.SemaphoreType.DMA((4, 16)),
         pltpu.SemaphoreType.DMA((4, 10)),
@@ -633,13 +731,16 @@
         pltpu.SemaphoreType.DMA((20,)),
         pltpu.SemaphoreType.DMA((20,)),
     ]
-    shapes = (((ROWS, D), BF16), ((ROWS, KV), BF16), ((RANK, OWN), F32), ((RANK, KV), F32))
+    grads = [((RANK, OWN), F32), ((RANK, KV), F32)]
+    shapes = [((ROWS, D), BF16), ((ROWS, KV), F32)] + grads
+    shapes += [((4, 1920, 128), BF16), ((RANK, 1920), BF16), ((ROWS, 1920), BF16)]
+    shapes += [((ROWS, KV), BF16), ((ROWS, RANK), BF16)]
     inputs = (lengths, tokens, cotangent, frozen, down_t, up_weight)
     results = pl.pallas_call(
         comm_kernel,
         out_shape=tuple(pltpu.VMEM(*shape) for shape in shapes),
         in_specs=[anywhere] * 6,
-        out_specs=(vmem,) * 4,
+        out_specs=(vmem,) * len(shapes),
         scratch_shapes=scratch,
         compiler_params=pltpu.CompilerParams(
             collective_id=0, has_side_effects=True, vmem_limit_bytes=46 * 1024 * 1024
@@ -647,14 +748,19 @@
         name="gather_multiply_sum",
     )(*[in_hbm(array) for array in inputs])
     results = [pltpu.with_memory_space_constraint(array, pltpu.VMEM) for array in results]
-    ig, keys, dgrad, ugrad = pl.pallas_call(
-        store_kernel,
-        out_shape=tuple(jax.ShapeDtypeStruct(*shape) for shape in shapes),
-        in_specs=[vmem] * 4,
+    outs = [((ROWS, KV), BF16), ((ROWS, D), BF16)] + grads
+    keys, ig, dgrad, ugrad = pl.pallas_call(
+        last_kernel,
+        out_shape=tuple(jax.ShapeDtypeStruct(*shape) for shape in outs),
+        in_specs=[vmem] * len(results),
         out_specs=(anywhere,) * 4,
-        scratch_shapes=[pltpu.SemaphoreType.DMA((PARTS + 3,))],
-        compiler_params=pltpu.CompilerParams(vmem_limit_bytes=4 * 1024 * 1024),
-        name="store",
+        scratch_shapes=[
+            pltpu.VMEM((ROWS, 1920), BF16),
+            pltpu.VMEM((ROWS, KV), BF16),
+            pltpu.SemaphoreType.DMA((9,)),
+        ],
+        compiler_params=pltpu.CompilerParams(vmem_limit_bytes=8 * 1024 * 1024),
+        name="last_products",
     )(*results)
     return keys, ig, dgrad.T, ugrad
 

time: 69.3 us -> 66.9 us (0.965)
  Pallas kernels: 68.3 us -> 66 us
    pallas_call x1, Pallas kernels: 65.1 us -> 62.7 us  [on_device(): pl.pallas_call(comm_kernel, out_shape=tuple((pltpu.VMEM(*shape) for shape...]
where the time goes in v3:
time: 66.9 us; the launch traced here: 66.8 us
  Pallas kernels  66 us (99%)
  between operations  0.8 us (1%)
    pallas_call x1, Pallas kernels, on_device(): pl.pallas_call(comm_kernel, out_shape=tuple((pltpu.VMEM(*shape) for shape...  62.7 us
    pallas_call x1, Pallas kernels, on_device(): pl.pallas_call(last_kernel, out_shape=tuple((jax.ShapeDtypeStruct(*shape)...  3.33 us

profile of v3, /device:TPU:1, one launch (start us, length us, event | category | flops | bytes accessed | tf_op | source)
XLA Modules:
  0.0 66.8 jit_solution(5686366448629305410)
XLA Ops:
  0.6 62.7 %gather_multiply_sum.1 = (bf16[256,14848]{1,0:T(8,128)(2,1)S(1)}, f32[256,512]{1,0:T(8,128)S(1)}, f32[64,116]{1,0:T(8,128)S(1)}, f32[64,512]{1,0:T(8,128)S(1)}, ...) custom-call(s32[8]{0:T(128)} %lengths_hbm.1, ...), custom_call_target="tpu_custom_call" | custom-call | tf_op jit(solution)/shard_map/gather_multiply_sum/pallas_call | solution.py:739
  63.3 3.3 %last_products.1 = (bf16[256,512]{1,0:T(8,128)(2,1)}, bf16[256,14848]{1,0:T(8,128)(2,1)}, f32[64,116]{1,0:T(8,128)}, f32[64,512]{1,0:T(8,128)}) custom-call(bf16[256,14848]{1,0:T(8,128)(2,1)S(1)} %get-tuple-element.17.ig, f32[256,512]{1,0:T(8,128)S(1)} %get-tuple-element.18.total, f32[64,116]{1,0:T(8,128)S(1)} %get-tuple-element.19.dgrad, ...), custom_call_target="tpu_custom_call" | custom-call | tf_op jit(solution)/shard_map/last_products/pallas_call | solution.py:752

commit v4 on v3

--- a/solution.py
+++ b/solution.py
@@ -16,9 +16,9 @@
 
 STREAMS = {
     "D": ("down", "yxz", 0, 64),
-    "Z": ("w", "xyz", 0, 160),
-    "X": ("w", "zyx", 160, 176),
-    "Y": ("w", "zxy", 336, 128),
+    "Z": ("w", "xyz", 0, 176),
+    "X": ("w", "zyx", 176, 176),
+    "Y": ("w", "zxy", 352, 112),
 }
 SUMS = (("xyz", 0, 24, 8), ("yzx", 24, 24, 16), ("zxy", 48, 16, 8))
 ALL = slice(None)
@@ -56,7 +56,7 @@
     lengths_hbm, tokens_hbm, cot_hbm, frozen_hbm, down_hbm, up_hbm,
     ig, total, dgrad, ugrad, w_last, dt_last, tokens_last, masked, raised_out,
     w, dt, tokens, lengths, cot, frozen, down_t, up,
-    stage, quad, dt_raw, g, r, x0, sa, sb, sl, sr, sy, xa, xb, xl, xr, y2, y3, u0, u1, u2, u3,
+    stage, quad, dt_raw, g, r, x0, sa, sb, sl, sr, sy, xa, xb, xl, xr, y2, y3, u0, u1, u2, u3, low_sum,
     load_sem, quad_s, quad_r, ag_s, ag_r, sib_s, sib_r, rs_s, rs_r, up_s, up_r,
 ):
     outer, inner = lax.axis_index("outer"), lax.axis_index("inner")
@@ -396,18 +396,23 @@
                 piece = dt_raw[c // 2, 2 * (c % 2) + o // 2, o % 2, x, zhi]
                 dt[:, OWN * i + STEP * c : OWN * (i + 1) + STEP * c] = piece[:, 0:OWN]
 
-    def low():
-        base, size = rows_of(me, 3, 1)
-        at = pl.ds(pl.multiple_of(base, 128), size)
-        dt_last[...] = dt[:, at]
-        tokens_last[...] = tokens[:, at]
-        low = jnp.zeros((ROWS, RANK), F32)
-        for c in range(29):
-            low += lax.dot_general(
+    def low(part):
+        if part == 0:
+            base, size = rows_of(me, 3, 1)
+            at = pl.ds(pl.multiple_of(base, 128), size)
+            dt_last[...] = dt[:, at]
+            tokens_last[...] = tokens[:, at]
+        first, last = (0, 8, 15, 22, 29)[part : part + 2]
+        out = jnp.zeros((ROWS, RANK), F32) if part == 0 else low_sum[...]
+        for c in range(first, last):
+            out += lax.dot_general(
                 tokens[:, 512 * c : 512 * (c + 1)], dt[:, 512 * c : 512 * (c + 1)], CONTRACT,
                 preferred_element_type=F32,
             )
-        lowered2 = low.astype(BF16) * jnp.asarray(adapter_scale, BF16)
+        if part < 3:
+            low_sum[...] = out
+            return
+        lowered2 = out.astype(BF16) * jnp.asarray(adapter_scale, BF16)
         lowered2_t = lowered2.astype(F32).T.astype(BF16)
         u0[...] = jnp.dot(lowered2_t, masked[...], preferred_element_type=F32)
         state["k"] = []
@@ -480,153 +485,157 @@
     enter()
     owners_pair(0)
     D_.open1()
+    D_.open2(0)
     exchange()
     owners(2)
     owners(3)
     owners_pair(3)
-    D_.open2(0)
     owners_pair(2)
     owners(1)
+    D_.open30(2)
     owners_pair(1)
-    D_.open30(2)
+    D_.open30(1)
     D_.open2(1)
-    D_.open30(1)
     D_.open2(2)
-    D_.open30(0)
     D_.open30(3)
     D_.open2(3)
     D_.close1()
+    D_.open30(0)
     piece()
     Z_.open1()
-    Z_.open2(0)
     Y_.open1()
     Y_.open2(0)
     Y_.open30(0)
+    Z_.open2(0)
     X_.open1()
     X_.open2(0)
+    Z_.open30(0)
+    X_.open30(0)
     add_siblings()
     sums[1].first()
-    X_.open30(0)
+    sums[2].first()
+    sums[0].first()
     D_.fwd3("P", 0)
     D_.fwd3("O", 0)
     D_.fwd2("P")
     D_.fwd2("O")
     D_.open3(2)
     D_.open3(1)
-    sums[0].first()
     Y_.open2(1)
     Y_.open30(1)
     Y_.open2(2)
+    Y_.open30(2)
     D_.close2()
     D_.open3(3)
-    Y_.open30(2)
     Z_.open2(1)
     Z_.open2(2)
+    Y_.open30(3)
     Y_.open2(3)
     Y_.close1()
     X_.open2(1)
     X_.open2(2)
+    X_.open30(1)
+    X_.open30(2)
     Z_.open2(3)
     Z_.close1()
-    X_.open30(1)
+    Z_.open30(2)
     X_.open2(3)
+    X_.open30(3)
     X_.close1()
+    Z_.open30(3)
+    sums[2].second()
+    sums[1].second()
     D_.close3(0)
-    X_.open30(3)
-    sums[2].first()
-    Z_.open30(2)
-    D_.fwd3("P", 2)
-    D_.fwd3("O", 2)
-    X_.open30(2)
     sums[0].second()
     Y_.fwd2("P")
     Z_.open30(1)
+    D_.fwd3("P", 2)
+    D_.fwd3("O", 2)
+    Y_.fwd3("O", 0)
+    Y_.fwd2("O")
+    Y_.fwd3("P", 0)
+    D_.fwd3("P", 1)
     D_.fwd3("O", 1)
-    D_.fwd3("P", 1)
-    Y_.open30(3)
-    Y_.fwd2("O")
     Y_.open3(1)
+    X_.fwd3("P", 0)
     D_.fwd3("P", 3)
     D_.fwd3("O", 3)
-    sums[2].second()
-    X_.fwd3("P", 0)
     Z_.fwd2("O")
+    X_.fwd3("O", 0)
     Z_.fwd2("P")
-    X_.fwd3("O", 0)
+    Z_.open3(1)
     X_.fwd2("O")
-    D_.close3(2)
-    Z_.open30(3)
     X_.fwd2("P")
-    Y_.fwd3("O", 0)
-    Z_.open30(0)
-    Y_.fwd3("P", 0)
     X_.open3(1)
-    D_.close3(1)
     sums[0].third()
-    Z_.open3(1)
-    D_.close3(3)
-    Y_.close2()
-    Y_.fwd3("O", 1)
-    low_rows()
-    X_.close3(0)
-    Y_.fwd3("P", 1)
     X_.open3(2)
     sums[2].third()
+    Z_.open3(2)
+    Y_.close2()
+    sums[1].third()
     Z_.fwd3("P", 0)
     Z_.fwd3("O", 0)
-    low()
+    D_.close3(2)
+    Y_.close3(0)
+    D_.close3(1)
+    X_.close3(0)
+    Y_.open3(2)
+    D_.close3(3)
+    Y_.fwd3("O", 1)
+    keys_part(0, 0)
+    Y_.fwd3("P", 1)
+    low_rows()
+    low(0)
     X_.fwd3("P", 1)
-    X_.close2()
-    Y_.open3(2)
-    Z_.open3(2)
-    Z_.close2()
-    keys_part(0, 0)
+    low(1)
     X_.fwd3("O", 1)
+    Y_.open3(3)
+    low(2)
+    low(3)
     Z_.fwd3("P", 1)
     Z_.fwd3("O", 1)
+    X_.close2()
+    X_.open3(3)
+    Z_.close2()
     input_part(0, 0)
-    Y_.open3(3)
+    X_.fwd3("P", 2)
+    Z_.open3(3)
     sums[0].fourth()
+    X_.fwd3("O", 2)
+    Z_.fwd3("P", 2)
+    Z_.fwd3("O", 2)
+    Y_.fwd3("O", 2)
+    sums[2].fourth()
+    Y_.fwd3("P", 2)
+    sums[1].fourth()
+    X_.close3(1)
+    Y_.close3(1)
     Z_.close3(0)
-    Y_.close3(0)
-    Y_.close3(1)
-    X_.open3(3)
+    Y_.fwd3("O", 3)
     up_x()
-    X_.fwd3("P", 2)
     keys_part(0, 1)
-    X_.fwd3("O", 2)
-    sums[1].second()
+    Y_.fwd3("P", 3)
+    X_.fwd3("P", 3)
     input_part(0, 1)
-    Y_.fwd3("O", 2)
-    Y_.fwd3("P", 2)
-    Z_.open3(3)
-    sums[2].fourth()
-    Z_.fwd3("O", 2)
-    Z_.fwd3("P", 2)
-    X_.close3(1)
-    Y_.fwd3("O", 3)
-    Y_.fwd3("P", 3)
     Z_.close3(1)
+    X_.fwd3("O", 3)
+    keys_part(1, 0)
+    sums[2].fifth()
+    input_part(1, 0)
+    X_.close3(2)
+    keys_part(1, 1)
+    sums[1].fifth()
+    up_y()
+    Z_.fwd3("O", 3)
+    Z_.fwd3("P", 3)
+    input_part(1, 1)
+    keys_part(2, 0)
+    X_.close3(3)
+    Z_.close3(2)
     sums[0].fifth()
-    keys_part(1, 0)
-    sums[1].third()
-    X_.fwd3("P", 3)
-    X_.fwd3("O", 3)
-    input_part(1, 0)
-    up_y()
-    keys_part(1, 1)
-    sums[2].fifth()
-    Z_.fwd3("P", 3)
-    X_.close3(2)
-    Z_.fwd3("O", 3)
-    input_part(1, 1)
-    Z_.close3(2)
+    input_part(2, 0)
     Y_.close3(2)
     Y_.close3(3)
-    keys_part(2, 0)
-    input_part(2, 0)
-    X_.close3(3)
-    sums[1].fourth()
     up_gather()
     keys_part(2, 1)
     input_part(2, 1)
@@ -634,7 +643,6 @@
     keys_part(3, 0)
     input_part(3, 0)
     last_rows()
-    sums[1].fifth()
     wait_up()
     for s in streams.values():
         need(*s.copies.values(), *s.sibs.values())
@@ -719,6 +727,7 @@
         pltpu.VMEM((7, 8, KV), F32),
         pltpu.VMEM((4, 8, KV), F32),
         pltpu.VMEM((4, 8, KV), F32),
+        pltpu.VMEM((ROWS, RANK), F32),
         pltpu.SemaphoreType.DMA((9,)),
         pltpu.SemaphoreType.DMA((3,)),
         pltpu.SemaphoreType.DMA((3,)),

time: 66.9 us -> 65.9 us (0.985)
  Pallas kernels: 66 us -> 65 us
    pallas_call x1, Pallas kernels: 62.7 us -> 61.6 us  [on_device(): pl.pallas_call(comm_kernel, out_shape=tuple((pltpu.VMEM(*shape) for shape...]
where the time goes in v4:
time: 65.9 us; the launch traced here: 65.8 us
  Pallas kernels  65 us (99%)
  between operations  0.8 us (1%)
    pallas_call x1, Pallas kernels, on_device(): pl.pallas_call(comm_kernel, out_shape=tuple((pltpu.VMEM(*shape) for shape...  61.6 us
    pallas_call x1, Pallas kernels, on_device(): pl.pallas_call(last_kernel, out_shape=tuple((jax.ShapeDtypeStruct(*shape)...  3.33 us

profile of v4, /device:TPU:1, one launch (start us, length us, event | category | flops | bytes accessed | tf_op | source)
XLA Modules:
  0.0 65.8 jit_solution(10217819975686755666)
XLA Ops:
  0.6 61.6 %gather_multiply_sum.1 = (bf16[256,14848]{1,0:T(8,128)(2,1)S(1)}, f32[256,512]{1,0:T(8,128)S(1)}, f32[64,116]{1,0:T(8,128)S(1)}, f32[64,512]{1,0:T(8,128)S(1)}, ...) custom-call(s32[8]{0:T(128)} %lengths_hbm.1, ...), custom_call_target="tpu_custom_call" | custom-call | tf_op jit(solution)/shard_map/gather_multiply_sum/pallas_call | solution.py:748
  62.3 3.3 %last_products.1 = (bf16[256,512]{1,0:T(8,128)(2,1)}, bf16[256,14848]{1,0:T(8,128)(2,1)}, f32[64,116]{1,0:T(8,128)}, f32[64,512]{1,0:T(8,128)}) custom-call(bf16[256,14848]{1,0:T(8,128)(2,1)S(1)} %get-tuple-element.17.ig, f32[256,512]{1,0:T(8,128)S(1)} %get-tuple-element.18.total, f32[64,116]{1,0:T(8,128)S(1)} %get-tuple-element.19.dgrad, ...), custom_call_target="tpu_custom_call" | custom-call | tf_op jit(solution)/shard_map/last_products/pallas_call | solution.py:761
